TPU v7x, 512 devices: a whole 4x4x16 slice. The times are simulated.
512 devices in a mesh: replica: 32 (over x, y, core), expert: 16 (over z).
Axes of the slice: x: 4, y: 4, z: 16, core: 2. Of those that a mesh axis runs over, the one named last changes fastest.
Arguments:
- queries: bfloat16 [1024, 4096], P(('replica', 'expert'))
- fresh_key_value: bfloat16 [1024, 512], P(('replica', 'expert')), may hold values from -6 to 6
- resid: bfloat16 [1024, 4096], P(('replica', 'expert')), may hold values from -6 to 6
- norm_gain: float32 [4096], replicated, may hold values from 0.5 to 1.5
- res_cache: bfloat16 [512, 128, 512], P(('replica', 'expert'))
- res_len: int32 [512], P(('replica', 'expert')), may hold values from 2 to 128
- long_cache: bfloat16 [512, 256, 512], P(('replica', 'expert'))
- long_len: int32 [32, 16], P(None, 'expert'), may hold values from 2 to 256
- migrate_from: int32 [32, 16], P(None, 'expert'), may hold values from 0 to 31, as said below
- expert_ids: int32 [1024, 8], P(('replica', 'expert')), may hold values from 0 to 63, as said below
- gate_wts: float32 [1024, 8], P(('replica', 'expert')), may hold values from 0.05 to 0.4
- w_gate: bfloat16 [98304, 4096], P(('expert', 'replica')), may hold values from -0.09375 to 0.09375
- w_up: bfloat16 [98304, 4096], P(('expert', 'replica')), may hold values from -0.09375 to 0.09375
- w_down: bfloat16 [64, 1536, 4096], P('expert', None, 'replica'), may hold values from -0.15625 to 0.15625
Outputs:
- attn_out: bfloat16 [1024, 4096], P(('replica', 'expert'))
- layer_out: bfloat16 [1024, 4096], P(('replica', 'expert'))
Inputs may be any that keep to these rules, and one draw needn't show every extreme that they name: For each expert index e, migrate_from[:, e] is a permutation of the replica indices. `expert_ids`: the 16 picks of one device name different experts; at most 2 of them lie in one expert index's experts (x // 4); in every draw, for some replica index, some expert index receives exactly 2 picks from every device of that replica index.
All inputs are finite; a program needn't handle non-finite values.
Results may differ from a plain program's by a relative error of at most 0.015.
Values may be sent and summed in bfloat16 or wider, within the bound.
No kernel may reach another device: no remote copies, remote signals or barrier semaphores. Data moves between devices by JAX's collectives and lax.ppermute only.
A program may use at most 64 MiB of HBM per device.

v0:
```python
import math

import jax
import jax.numpy as jnp
from jax import lax
from jax.sharding import PartitionSpec as P

QUERY_HEADS = 32
KEY_VALUE_HEADS = 2
HEAD_SIZE = 128
EXP_DEV = 4
FFW = 1536


def partial_softmax(query_vector, block_tile, valid):
    row_list = query_vector.shape[0]
    count_number = block_tile.shape[1]
    head_group = QUERY_HEADS // KEY_VALUE_HEADS
    head_list = query_vector.reshape(row_list, KEY_VALUE_HEADS, head_group, HEAD_SIZE)
    key_rows = block_tile[:, :, : KEY_VALUE_HEADS * HEAD_SIZE].reshape(
        row_list, count_number, KEY_VALUE_HEADS, HEAD_SIZE
    )
    value_rows = block_tile[:, :, KEY_VALUE_HEADS * HEAD_SIZE :].reshape(
        row_list, count_number, KEY_VALUE_HEADS, HEAD_SIZE
    )
    scores = jnp.einsum(
        "rkgd,rnkd->rkgn", head_list, key_rows, preferred_element_type=jnp.float32
    ) * (1.0 / math.sqrt(HEAD_SIZE))
    live = valid[:, None, None, :]
    scores = jnp.where(live, scores, -1e30)
    peak = jnp.max(scores, axis=-1)
    weights = jnp.where(live, jnp.exp(scores - peak[..., None]), 0.0).astype(jnp.bfloat16)
    weights = lax.optimization_barrier(weights)
    total = jnp.sum(weights.astype(jnp.float32), axis=-1)
    summed = jnp.einsum("rkgn,rnkd->rkgd", weights, value_rows, preferred_element_type=jnp.float32)
    return (
        peak.reshape(row_list, QUERY_HEADS),
        total.reshape(row_list, QUERY_HEADS),
        summed.reshape(row_list, QUERY_HEADS, HEAD_SIZE),
    )


def combine(first, second):
    peak = jnp.maximum(first[0], second[0])
    left = jnp.exp(first[0] - peak)
    right = jnp.exp(second[0] - peak)
    return (
        peak,
        first[1] * left + second[1] * right,
        first[2] * left[..., None] + second[2] * right[..., None],
    )


def finish(state):
    return (state[2] / state[1][..., None]).reshape(state[2].shape[0], QUERY_HEADS * HEAD_SIZE)


def slot_table(picked, owners, capacity, per_owner):
    owner = picked // per_owner
    local = picked - owner * per_owner
    count_number = picked.shape[-1]
    same = owner[..., :, None] == owner[..., None, :]
    earlier = jnp.arange(count_number)[:, None] > jnp.arange(count_number)[None, :]
    rank = jnp.sum(same & earlier, axis=-1)
    target = owner * capacity + rank
    onehot = jnp.arange(owners * capacity)[:, None] == target[..., None, :]
    labels = jnp.sum(jnp.where(onehot, local[..., None, :] + 1, 0), axis=-1) - 1
    return (onehot, labels)


def on_device(
    queries,
    fresh_key_value,
    resid,
    norm_gain,
    res_cache,
    res_len,
    long_cache,
    long_len,
    migrate_from,
    expert_ids,
    gate_wts,
    w_gate,
    w_up,
    w_down,
):
    replicas = lax.axis_size("replica")
    owners = lax.axis_size("expert")
    myself = lax.axis_index("replica")
    single = jnp.ones((1, 1), dtype=bool)
    own_valid = (jnp.arange(res_cache.shape[1]) < res_len[0])[None, :]
    own_state = combine(
        partial_softmax(queries[0:1], res_cache, own_valid),
        partial_softmax(queries[0:1], fresh_key_value[0:1][:, None, :], single),
    )
    piece = long_cache.shape[1] // replicas
    slices = long_cache.reshape(replicas, piece, long_cache.shape[2])
    source_of = migrate_from[:, 0]
    lengths = long_len[:, 0]
    spread = lax.all_to_all(slices, "replica", split_axis=0, concat_axis=0, tiled=True)
    by_target = jnp.take(spread, source_of, axis=0)
    arrived_cache = lax.all_to_all(by_target, "replica", split_axis=0, concat_axis=0, tiled=True)
    arrived_cache = arrived_cache.reshape(1, replicas * piece, long_cache.shape[2])
    root = migrate_from[myself, 0]
    filled = lengths[root]
    guest_valid = (jnp.arange(replicas * piece) < filled)[None, :]
    guest_state = partial_softmax(queries[1:2], arrived_cache, guest_valid)
    guest_state = combine(
        guest_state, partial_softmax(queries[1:2], fresh_key_value[1:2][:, None, :], single)
    )
    attn_out = jnp.concatenate([finish(own_state), finish(guest_state)], axis=0).astype(
        jnp.bfloat16
    )
    stream = resid.astype(jnp.float32) + attn_out.astype(jnp.float32)
    normed = (
        stream * lax.rsqrt(jnp.mean(stream * stream, axis=-1, keepdims=True) + 1e-06) * norm_gain
    ).astype(jnp.bfloat16)
    per_owner = EXP_DEV
    top = expert_ids.shape[1]
    capacity = max(2, 2 * top // owners)
    width_extent = normed.shape[1]
    own_onehot, own_labels = slot_table(expert_ids.reshape(-1), owners, capacity, per_owner)
    picks = jnp.repeat(normed, top, axis=0)
    outgoing = jnp.dot(own_onehot.astype(jnp.bfloat16), picks, preferred_element_type=jnp.float32)
    outgoing = outgoing.astype(jnp.bfloat16).reshape(owners, capacity, width_extent)
    tags = own_labels.astype(jnp.bfloat16).reshape(owners, capacity)
    incoming, tags_in = (
        lax.all_to_all(outgoing, "expert", split_axis=0, concat_axis=0, tiled=True),
        lax.all_to_all(tags, "expert", split_axis=0, concat_axis=0, tiled=True),
    )
    tokens, labels = (
        lax.all_gather(incoming, "replica", axis=0, tiled=True),
        lax.all_gather(tags_in, "replica", axis=0, tiled=True),
    )
    tokens = tokens.reshape(-1, width_extent)
    labels = labels.reshape(-1).astype(jnp.int32)
    share = w_gate.shape[0]
    start_row = myself * share
    local_expert = start_row // FFW
    first_unit = start_row - local_expert * FFW
    gate = jnp.einsum("md,fd->mf", tokens, w_gate, preferred_element_type=jnp.float32)
    up = jnp.einsum("md,fd->mf", tokens, w_up, preferred_element_type=jnp.float32)
    mine = labels == local_expert
    act = jnp.where(mine[:, None], jax.nn.silu(gate) * up, 0.0).astype(jnp.bfloat16)
    placed = lax.dynamic_update_slice(
        jnp.zeros((tokens.shape[0], FFW), jnp.float32), act.astype(jnp.float32), (0, first_unit)
    )
    hidden = lax.psum(placed.astype(jnp.bfloat16), "replica")
    contrib = jnp.einsum("mf,xfd->mxd", hidden, w_down, preferred_element_type=jnp.float32)
    select = labels[:, None] == jnp.arange(per_owner)[None, :]
    produced = jnp.sum(jnp.where(select[:, :, None], contrib, 0.0), axis=1).astype(jnp.bfloat16)
    shaped = produced.reshape(replicas, owners, capacity, -1)
    back = lax.all_to_all(
        lax.all_to_all(shaped, "replica", split_axis=0, concat_axis=3, tiled=True),
        "expert",
        split_axis=1,
        concat_axis=0,
        tiled=True,
    )
    back = back.reshape(owners * capacity, width_extent)
    weighted = jnp.where(own_onehot, gate_wts.reshape(-1)[None, :], 0.0)
    per_row = weighted.reshape(owners * capacity, 2, top).sum(axis=-1).T
    mixture = jnp.dot(per_row, back.astype(jnp.float32), precision=lax.Precision.HIGHEST)
    layer_out = (stream + mixture).astype(jnp.bfloat16)
    return (attn_out, layer_out)


def solution(mesh):
    placed = (
        P(("replica", "expert"), None),
        P(("replica", "expert"), None),
        P(("replica", "expert"), None),
        P(),
        P(("replica", "expert"), None, None),
        P(("replica", "expert")),
        P(("replica", "expert"), None, None),
        P(None, "expert"),
        P(None, "expert"),
        P(("replica", "expert"), None),
        P(("replica", "expert"), None),
        P(("expert", "replica"), None),
        P(("expert", "replica"), None),
        P("expert", None, "replica"),
    )
    return jax.shard_map(
        on_device,
        mesh=mesh,
        in_specs=placed,
        out_specs=(P(("replica", "expert"), None), P(("replica", "expert"), None)),
        check_vma=False,
    )
```

profile of v0, /device:TPU:32, one launch (start us, length us, event | category | flops | bytes accessed | tf_op | source)
XLA Modules:
  0.0 368.7 jit_solution(16550842318986357969)
XLA Ops:
  7.2 7.5 %all-to-all-start = ((bf16[32,8,512]{2,1,0:T(8,128)(2,1)}), bf16[32,8,512]{2,1,0:T(8,128)(2,1)S(1)}, u32[]{:S(2)}, u32[]{:S(2)}) async-start(bf16[32,8,512]{2,1,0:T(8,128)(2,1)} %bitcast.101), calls=%async_computation | async-start | bytes 524288 | tf_op jit(solution)/shard_map/all_to_all | solution.py:100
  14.7 0.7 fusion.31
  15.3 0.7 and_bitcast_fusion
  16.0 0.9 slice_reduce_fusion.1
  16.9 0.8 slice_bitcast_fusion.1
  17.6 0.1 fusion.24
  17.9 0.1 fusion.23
  18.0 0.9 fusion.37
  18.9 0.1 copy.81
  19.7 0.2 fusion.39
  20.3 0.1 copy.82
  20.5 0.1 fusion.19
  20.6 0.8 reshape.764
  21.4 0.2 convert_reduce_fusion.3
  21.9 1.2 constant_dynamic-slice_fusion.1
  25.1 1.2 constant_dynamic-slice_fusion
  26.4 0.6 gather_fusion
  27.0 0.8 broadcast_select_fusion
  27.7 7.4 %all-to-all-start.1 = ((bf16[32,8,512]{2,1,0:T(8,128)(2,1)}), bf16[32,8,512]{2,1,0:T(8,128)(2,1)S(1)}, u32[]{:S(2)}, u32[]{:S(2)}) async-start(bf16[32,8,512]{2,1,0:T(8,128)(2,1)} %broadcast_select_fusion), calls=%async_computation.1 | async-start | bytes 524288 | tf_op jit(solution)/shard_map/all_to_all | solution.py:102
  35.2 0.7 iota_compare_fusion.5
  36.1 8.0 %all-to-all-done.1 = bf16[32,8,512]{2,1,0:T(8,128)(2,1)S(1)} async-done(((bf16[32,8,512]{2,1,0:T(8,128)(2,1)}), bf16[32,8,512]{2,1,0:T(8,128)(2,1)S(1)}, u32[]{:S(2)}, u32[]{:S(2)}) %all-to-all-start.1) | async-done | bytes 262176 | tf_op jit(solution)/shard_map/all_to_all | solution.py:102
  44.2 0.2 fusion.38
  44.9 0.1 fusion.14
  45.3 0.2 multiply_reduce_fusion
  45.6 0.3 convolution_convert_fusion
  45.9 0.2 reshape.766
  46.1 33.6 %all_to_all.51 = bf16[16,2,4096]{2,1,0:T(2,128)(2,1)} all-to-all(bf16[16,2,4096]{2,1,0:T(2,128)(2,1)S(1)} %reshape.766), channel_id=1, replica_groups=mesh['replica'=32,'expert'=16] {'expert'}, dimensions={0} | all-to-all | bytes 524288 | tf_op jit(solution)/shard_map/all_to_all | solution.py:128
  79.9 0.7 convert_element_type.123
  80.6 6.1 %all-to-all-start.2 = ((bf16[16,1,2]{2,1,0:T(2,128)(2,1)}), bf16[16,1,2]{2,1,0:T(2,128)(2,1)S(1)}, u32[]{:S(2)}, u32[]{:S(2)}) async-start(bf16[16,1,2]{2,1,0:T(2,128)(2,1)} %convert_element_type.123), calls=%async_computation.2 | async-start | bytes 16384 | tf_op jit(solution)/shard_map/all_to_all | solution.py:129
  86.8 11.0 %all-to-all-done.2 = bf16[16,1,2]{2,1,0:T(2,128)(2,1)S(1)} async-done(((bf16[16,1,2]{2,1,0:T(2,128)(2,1)}), bf16[16,1,2]{2,1,0:T(2,128)(2,1)S(1)}, u32[]{:S(2)}, u32[]{:S(2)}) %all-to-all-start.2) | async-done | bytes 96 | tf_op jit(solution)/shard_map/all_to_all | solution.py:129
  97.8 23.1 %all-gather = bf16[512,1,2]{2,1,0:T(2,128)(2,1)S(1)} all-gather(bf16[16,1,2]{2,1,0:T(2,128)(2,1)S(1)} %all-to-all-done.2), channel_id=2, replica_groups=mesh['replica'=32,'expert'=16] {'replica'}, dimensions={0}, use_global_device_ids=true | all-gather | bytes 2112 | tf_op jit(solution)/shard_map/all_gather | solution.py:133
  120.9 0.8 convert_reduce_fusion
  121.7 0.2 reshape.777
  121.9 17.5 %all-gather.3.cloned.1.call-done = bf16[512,2,4096]{2,1,0:T(2,128)(2,1)} async-done(((bf16[16,2,4096]{2,1,0:T(2,128)(2,1)}), bf16[512,2,4096]{2,1,0:T(2,128)(2,1)}) %all-gather.3.cloned.1.call-update) | async-done | bytes 8388624 | tf_op jit(solution)/shard_map/all_gather | solution.py:132
  139.4 13.1 %reshape.767 = bf16[1024,4096]{1,0:T(8,128)(2,1)} reshape(bf16[512,2,4096]{2,1,0:T(2,128)(2,1)} %all-gather.3.cloned.1.call-done) | data formatting | bytes 16777216 | tf_op jit(solution)/shard_map/reshape | solution.py:135
  152.5 6.4 %fusion.40 = f32[1024,192]{0,1:T(8,128)S(1)} fusion(bf16[1024,4096]{1,0:T(8,128)(2,1)} %reshape.767, bf16[192,4096]{1,0:T(8,128)(2,1)S(1)} %copy-done), kind=kOutput, calls=%fused_computation.103 | convolution fusion | flops 1610612736 | bytes 10747904 | tf_op jit(solution)/shard_map/md,fd->mf/dot_general | solution.py:141
  159.0 3.0 fusion.7
  161.9 0.2 copy.68
  162.2 1.9 broadcast_in_dim.167
  164.1 5.6 %dynamic_update_slice.3 = bf16[1024,1536]{1,0:T(8,128)(2,1)} dynamic-update-slice(bf16[1024,1536]{1,0:T(8,128)(2,1)} %broadcast_in_dim.167, bf16[1024,192]{1,0:T(8,128)(2,1)S(1)} %copy.68, s32[]{:T(128)} %constant.41.clone.1, s32[]{:T(128)S(6)} %select_n.109) | dynamic-update-slice | bytes 786436 | tf_op jit(solution)/shard_map/dynamic_update_slice | solution.py:145
  169.7 141.0 %all-reduce.2.cloned.1.call-done = bf16[1024,1536]{1,0:T(8,128)(2,1)} async-done(((bf16[1024,1536]{1,0:T(8,128)(2,1)}), bf16[1024,1536]{1,0:T(8,128)(2,1)}) %all-reduce.2.cloned.1.call-update) | async-done | bytes 3145744 | tf_op jit(solution)/shard_map/psum | solution.py:148
  310.7 3.9 %select_reduce_fusion = bf16[1024,128]{1,0:T(8,128)(2,1)S(1)} fusion(bf16[4,1536,128]{2,1,0:T(8,128)(2,1)} %param.27, bf16[1024,1536]{1,0:T(8,128)(2,1)} %all-reduce.2.cloned.1.call-done, pred[1024,4]{0,1:T(4,128)(4,1)S(1)} %iota_compare_fusion), kind=kOutput, calls=%fused_computation.6 | convolution fusion | flops 1611530240 | bytes 4984832 | tf_op jit(solution)/shard_map/mf,xfd->mxd/dot_general | solution.py:149
  314.7 14.2 %all_to_all.52 = bf16[32,16,2,128]{3,2,1,0:T(2,128)(2,1)S(1)} all-to-all(bf16[32,16,2,128]{3,2,1,0:T(2,128)(2,1)S(1)} %bitcast.102), channel_id=1, replica_groups=mesh['replica'=32,'expert'=16] {'replica'}, dimensions={0} | all-to-all | bytes 524288 | tf_op jit(solution)/shard_map/all_to_all | solution.py:154
  328.9 0.1 copy.79
  329.0 0.8 reshape.796
  329.7 12.7 %all-to-all-start.5 = ((bf16[1,16,2,4096]{3,2,0,1:T(2,128)(2,1)}), bf16[1,16,2,4096]{3,2,0,1:T(2,128)(2,1)S(1)}, u32[]{:S(2)}, u32[]{:S(2)}) async-start(bf16[1,16,2,4096]{3,2,0,1:T(2,128)(2,1)} %reshape.796), calls=%async_computation.5 | async-start | bytes 524288 | tf_op jit(solution)/shard_map/all_to_all | solution.py:153
  342.6 18.3 %all-to-all-done.5 = bf16[1,16,2,4096]{3,2,0,1:T(2,128)(2,1)S(1)} async-done(((bf16[1,16,2,4096]{3,2,0,1:T(2,128)(2,1)}), bf16[1,16,2,4096]{3,2,0,1:T(2,128)(2,1)S(1)}, u32[]{:S(2)}, u32[]{:S(2)}) %all-to-all-start.5) | async-done | bytes 262176 | tf_op jit(solution)/shard_map/all_to_all | solution.py:153
  361.0 0.8 fusion
  (67 shorter events, 2.6 us)
Async XLA Ops:
  7.2 145.3 %copy-start = (bf16[192,4096]{1,0:T(8,128)(2,1)S(1)}, bf16[192,4096]{1,0:T(8,128)(2,1)}, u32[]{:S(2)}) copy-start(bf16[192,4096]{1,0:T(8,128)(2,1)} %param.25) | copy-start | bytes 4718596
  7.2 19.2 %all-to-all-start = ((bf16[32,8,512]{2,1,0:T(8,128)(2,1)}), bf16[32,8,512]{2,1,0:T(8,128)(2,1)S(1)}, u32[]{:S(2)}, u32[]{:S(2)}) async-start(bf16[32,8,512]{2,1,0:T(8,128)(2,1)} %bitcast.101), calls=%async_computation | async-start | bytes 524288 | tf_op jit(solution)/shard_map/all_to_all | solution.py:100
  18.0 27.3 %copy-start.2 = (bf16[2,4096]{1,0:T(2,128)(2,1)S(1)}, bf16[2,4096]{1,0:T(2,128)(2,1)}, u32[]{:S(2)}) copy-start(bf16[2,4096]{1,0:T(2,128)(2,1)} %param.16) | copy-start | bytes 49156
  18.0 27.5 %copy-start.4 = (f32[4096]{0:T(1024)S(1)}, f32[4096]{0:T(1024)}, u32[]{:S(2)}) copy-start(f32[4096]{0:T(1024)} %param.17) | copy-start | bytes 49156
  27.7 16.3 %all-to-all-start.1 = ((bf16[32,8,512]{2,1,0:T(8,128)(2,1)}), bf16[32,8,512]{2,1,0:T(8,128)(2,1)S(1)}, u32[]{:S(2)}, u32[]{:S(2)}) async-start(bf16[32,8,512]{2,1,0:T(8,128)(2,1)} %broadcast_select_fusion), calls=%async_computation.1 | async-start | bytes 524288 | tf_op jit(solution)/shard_map/all_to_all | solution.py:102
  35.1 104.3 %all-gather.3.cloned.1.call-start = ((), (), s32[]{:S(2)}) async-start(), calls=%async_computation.6 | async-start | bytes 8650752 | tf_op jit(solution)/shard_map/all_gather | solution.py:132
  45.5 315.5 %copy-start.3 = (bf16[2,4096]{1,0:T(2,128)(2,1)}, bf16[2,4096]{1,0:T(2,128)(2,1)S(1)}, u32[]{:S(2)}) copy-start(bf16[2,4096]{1,0:T(2,128)(2,1)S(1)} %get-tuple-element.7) | copy-start | bytes 49156
  80.6 17.2 %all-to-all-start.2 = ((bf16[16,1,2]{2,1,0:T(2,128)(2,1)}), bf16[16,1,2]{2,1,0:T(2,128)(2,1)S(1)}, u32[]{:S(2)}, u32[]{:S(2)}) async-start(bf16[16,1,2]{2,1,0:T(2,128)(2,1)} %convert_element_type.123), calls=%async_computation.2 | async-start | bytes 16384 | tf_op jit(solution)/shard_map/all_to_all | solution.py:129
  86.7 224.0 %all-reduce.2.cloned.1.call-start = ((), (), s32[]{:S(2)}) async-start(), calls=%async_computation.7 | async-start | bytes 6291456 | tf_op jit(solution)/shard_map/psum | solution.py:148
  152.5 6.4 %copy-start.1 = (bf16[1024,4096]{1,0:T(8,128)(2,1)S(1)}, bf16[1024,4096]{1,0:T(8,128)(2,1)}, u32[]{:S(2)}) copy-start(bf16[1024,4096]{1,0:T(8,128)(2,1)} %reshape.767) | copy-start | bytes 25165828
  152.5 6.4 %copy-start.7 = (bf16[192,4096]{1,0:T(8,128)(2,1)S(1)}, bf16[192,4096]{1,0:T(8,128)(2,1)}, u32[]{:S(2)}) copy-start(bf16[192,4096]{1,0:T(8,128)(2,1)} %param.26) | copy-start | bytes 4718596
  314.7 27.8 %copy-start.5 = (s32[2,8]{1,0:T(2,128)S(1)}, s32[2,8]{1,0:T(2,128)}, u32[]{:S(2)}) copy-start(s32[2,8]{1,0:T(2,128)} %param.23) | copy-start | bytes 196
  314.7 27.8 %copy-start.6 = (f32[2,8]{1,0:T(2,128)S(1)}, f32[2,8]{1,0:T(2,128)}, u32[]{:S(2)}) copy-start(f32[2,8]{1,0:T(2,128)} %param.24) | copy-start | bytes 196
  329.7 31.2 %all-to-all-start.5 = ((bf16[1,16,2,4096]{3,2,0,1:T(2,128)(2,1)}), bf16[1,16,2,4096]{3,2,0,1:T(2,128)(2,1)S(1)}, u32[]{:S(2)}, u32[]{:S(2)}) async-start(bf16[1,16,2,4096]{3,2,0,1:T(2,128)(2,1)} %reshape.796), calls=%async_computation.5 | async-start | bytes 524288 | tf_op jit(solution)/shard_map/all_to_all | solution.py:153
Sparse Core Ops, SparseCore 0:
  79.9 59.4 all-gather.2
  169.8 140.8 all-reduce.1
where the time goes:
time: 370 us; the launch traced here: 369 us
  waiting for transfers between devices  196 us (53%)
  blocking collectives  70.9 us (19%)
  starting transfers between devices  33.7 us (9%)
  local copies, waits for them, and re-layouts  30.8 us (8%)
  between operations  17 us (5%)
  matrix products  15.4 us (4%)
  other arithmetic  4.91 us (1%)
    psum x1, waiting for transfers between devices, on_device(): hidden = lax.psum(placed.astype(jnp.bfloat16), 'replica')  141 us
    all_to_all x1, blocking collectives, on_device(): lax.all_to_all(outgoing, 'expert', split_axis=0, concat_axis=0, tiled=True)  33.6 us
    all_gather x1, blocking collectives, on_device(): lax.all_gather(tags_in, 'replica', axis=0, tiled=True)  23.1 us
    all_to_all x1, waiting for transfers between devices, on_device(): lax.all_to_all(lax.all_to_all(shaped, 'replica', split_axis=0, concat_axi...  18.3 us
    all_gather x1, waiting for transfers between devices, on_device(): lax.all_gather(incoming, 'replica', axis=0, tiled=True)  17.5 us
    all_to_all x1, blocking collectives, on_device(): lax.all_to_all(shaped, 'replica', split_axis=0, concat_axis=3, tiled=True)  14.2 us
    reshape x1, local copies, waits for them, and re-layouts, on_device(): tokens = tokens.reshape(-1, width_extent)  13.1 us
    all_to_all x1, starting transfers between devices, on_device(): lax.all_to_all(lax.all_to_all(shaped, 'replica', split_axis=0, concat_axi...  12.7 us
  transfers between devices with their start and end apart: 6, of which 5 were waited for; matrix products, arithmetic and copies ran while one was open for 3% of the time, Pallas kernels for 0%

commit v1 on v0

v1 whole, which is shorter than its diff:
```python
import functools
import math

import jax
import jax.numpy as jnp
from jax import lax
from jax.experimental import pallas as pl
from jax.experimental.pallas import tpu as pltpu
from jax.sharding import Mesh
from jax.sharding import PartitionSpec as P

HEADS = 32
GROUP = 16
HEAD = 128
D = 4096
FFW = 1536
LOCAL = 4
UNITS = 192
PLANE = ("x", "y", "c")
XY = ("x", "y")
ALL = ("x", "y", "c", "z")
VMEM = pl.BlockSpec(memory_space=pltpu.VMEM)
SMEM = pl.BlockSpec(memory_space=pltpu.SMEM)


def params(mib):
    return pltpu.CompilerParams(vmem_limit_bytes=mib << 20)


def attend(q, cache_ref, fresh, length):
    slots = cache_ref.shape[0]
    fresh = fresh.astype(jnp.float32)
    outs = []
    for g in range(2):
        qg = q[g * GROUP : (g + 1) * GROUP]
        keys = cache_ref[:, g * HEAD : (g + 1) * HEAD]
        values = cache_ref[:, (2 + g) * HEAD : (3 + g) * HEAD]
        scale = 1.0 / math.sqrt(HEAD)
        scores = lax.dot_general(
            qg, keys, (((1,), (1,)), ((), ())), preferred_element_type=jnp.float32
        )
        scores = scores * scale
        live = lax.broadcasted_iota(jnp.int32, (GROUP, slots), 1) < length
        scores = jnp.where(live, scores, -1e30)
        last = (
            jnp.sum(qg.astype(jnp.float32) * fresh[g : g + 1], axis=1, keepdims=True)
            * scale
        )
        peak = jnp.maximum(jnp.max(scores, axis=1, keepdims=True), last)
        weights = jnp.where(live, jnp.exp(scores - peak), 0.0).astype(jnp.bfloat16)
        end = jnp.exp(last - peak).astype(jnp.bfloat16).astype(jnp.float32)
        total = jnp.sum(weights.astype(jnp.float32), axis=1, keepdims=True) + end
        summed = jnp.dot(weights, values, preferred_element_type=jnp.float32)
        summed = summed + end * fresh[2 + g : 3 + g]
        outs.append(summed / total)
    return jnp.concatenate(outs, axis=0)


def resident_kernel(len_ref, q_ref, kv_ref, cache_ref, out_ref):
    out = attend(q_ref[...], cache_ref, kv_ref[...], len_ref[0])
    out_ref[...] = out.astype(jnp.bfloat16)


def guest_kernel(me_ref, from_ref, len_ref, asked_ref, cache_ref, out_ref):
    me = me_ref[0]

    def look(i, found):
        return jnp.where(from_ref[i] == me, i, found)

    target = lax.fori_loop(0, from_ref.shape[0], look, 0)
    asked = asked_ref[target]
    out = attend(asked[:32], cache_ref, asked[32:48][:4], len_ref[me])
    out = out.astype(jnp.bfloat16)
    for r in range(out_ref.shape[0]):
        out_ref[r] = out


def token_kernel(
    me_ref, from_ref, own_ref, back_ref, resid_ref, gain_ref, meta_ref, attn_ref, stream_ref, out_ref
):
    root = from_ref[me_ref[0]]
    rows = (own_ref[...], back_ref[root])
    for r in range(2):
        attn_ref[r] = rows[r]
        stream = resid_ref[r].astype(jnp.float32) + rows[r].astype(jnp.float32)
        stream_ref[r] = stream
        square = jnp.sum(jnp.sum(stream * stream, axis=1, keepdims=True), axis=0, keepdims=True)
        normed = (stream * lax.rsqrt(square / D + 1e-06) * gain_ref[...]).astype(jnp.bfloat16)
        for e in range(out_ref.shape[0]):
            out_ref[e, r * 32 : (r + 1) * 32] = normed
    for e in range(out_ref.shape[0]):
        out_ref[e, 64:80] = meta_ref[e]


def select_kernel(rows_ref, meta_ref, out_ref):
    meta = meta_ref[...]
    first = rows_ref[:, :D].astype(jnp.float32)
    second = rows_ref[:, D:].astype(jnp.float32)
    for x in range(LOCAL):
        pick = meta[:, 16 + x : 17 + x].astype(jnp.float32) > 0.5
        row = jnp.where(pick, second, first).astype(jnp.bfloat16)
        for y in range(4):
            out_ref[x * 4 + y, :, :D] = row
            out_ref[x * 4 + y, :, D:] = meta


def up_kernel(core_ref, rows_ref, ga_ref, ua_ref, gb_ref, ub_ref, out_ref, gate_ref):
    rows = rows_ref[:, :D]
    dims = (((1,), (1,)), ((), ()))

    def act(g_ref, u_ref):
        gate = lax.dot_general(rows, g_ref[...], dims, preferred_element_type=jnp.float32)
        up = lax.dot_general(rows, u_ref[...], dims, preferred_element_type=jnp.float32)
        return gate * (1.0 / (1.0 + jnp.exp(-gate))) * up

    own = act(ga_ref, ua_ref)
    other = act(gb_ref, ub_ref)
    even = core_ref[0] == 0
    both = jnp.where(
        even,
        jnp.concatenate([own, other], axis=1),
        jnp.concatenate([other, own], axis=1),
    ).astype(jnp.bfloat16)
    n = rows.shape[0]
    to = lax.broadcasted_iota(jnp.int32, (n, n), 0)
    at = lax.broadcasted_iota(jnp.int32, (n, n), 1)
    swap = jnp.where((to % 16) * 16 + to // 16 == at, 1.0, 0.0).astype(jnp.bfloat16)
    both = jnp.dot(swap, both, preferred_element_type=jnp.float32).astype(jnp.bfloat16)
    gate_ref[...] = jnp.dot(swap, rows_ref[:, D:], preferred_element_type=jnp.float32)
    for p in range(out_ref.shape[0]):
        out_ref[p] = both


def down_kernel(act_ref, wa_ref, wb_ref, gate_ref, out_ref):
    gates = gate_ref[...]
    width = 2 * UNITS
    sums = [0.0, 0.0]
    for x in range(LOCAL):
        total = 0.0
        for y in range(4):
            block = pl.ds(y * width, width)
            w = jnp.concatenate([wa_ref[x, block], wb_ref[x, block]], axis=1)
            total += jnp.dot(act_ref[x * 4 + y], w, preferred_element_type=jnp.float32)
        for r in range(2):
            j = r * LOCAL + x
            weight = gates[:, j : j + 1] + gates[:, 8 + j : 9 + j]
            sums[r] += weight * total
    for r in range(2):
        part = sums[r].astype(jnp.bfloat16)
        for z in range(16):
            out_ref[z, r] = part[z * 16 : (z + 1) * 16]


def exchange(a, axes):
    return lax.all_to_all(a, axes, split_axis=0, concat_axis=0, tiled=True)


def pick_table(expert_ids, gate_wts, owners):
    wanted = jnp.arange(owners * LOCAL).reshape(owners, 1, LOCAL, 1)
    hit = expert_ids[None, :, None, :] == wanted
    gates = jnp.sum(jnp.where(hit, gate_wts[None, :, None, :], 0.0), axis=-1)
    high = gates.astype(jnp.bfloat16)
    rest = (gates - high.astype(jnp.float32)).astype(jnp.bfloat16)
    second = jnp.any(hit[:, 1], axis=-1).astype(jnp.bfloat16)
    line = jnp.concatenate([high.reshape(owners, 8), rest.reshape(owners, 8), second], axis=1)
    return jnp.pad(line[:, None, :], ((0, 0), (0, 15), (0, 108)))


def on_device(
    queries,
    fresh_key_value,
    resid,
    norm_gain,
    res_cache,
    res_len,
    long_cache,
    long_len,
    migrate_from,
    expert_ids,
    gate_wts,
    w_gate,
    w_up,
    w_down,
):
    bf16, f32 = jnp.bfloat16, jnp.float32
    core = lax.axis_index("c").reshape(1)
    me = lax.axis_index(PLANE).reshape(1)
    owners = 16
    swap = lambda a: lax.ppermute(a, "c", [(0, 1), (1, 0)])

    q = queries.reshape(2, HEADS, HEAD)
    kv = fresh_key_value.reshape(2, 4, HEAD)
    ask = jnp.concatenate([q[1], jnp.pad(kv[1], ((0, 12), (0, 0)))], axis=0)
    asked = exchange(jnp.broadcast_to(ask[None], (32, 48, HEAD)), PLANE)

    gate_b, up_b, down_b = swap(w_gate), swap(w_up), swap(w_down)
    own = pl.pallas_call(
        resident_kernel,
        out_shape=jax.ShapeDtypeStruct((HEADS, HEAD), bf16),
        in_specs=[SMEM, VMEM, VMEM, VMEM],
        out_specs=VMEM,
        name="resident_attention",
    )(res_len, q[0], kv[0], res_cache[0])
    source = migrate_from.reshape(32)
    guest = pl.pallas_call(
        guest_kernel,
        out_shape=jax.ShapeDtypeStruct((32, HEADS, HEAD), bf16),
        in_specs=[SMEM, SMEM, SMEM, VMEM, VMEM],
        out_specs=VMEM,
        name="guest_attention",
    )(me, source, long_len.reshape(32), asked, long_cache[0])
    back = exchange(guest, PLANE)
    meta = pick_table(expert_ids, gate_wts, owners)
    attn, stream, tokens = pl.pallas_call(
        token_kernel,
        out_shape=(
            jax.ShapeDtypeStruct((2, HEADS, HEAD), bf16),
            jax.ShapeDtypeStruct((2, HEADS, HEAD), f32),
            jax.ShapeDtypeStruct((owners, 80, HEAD), bf16),
        ),
        in_specs=[SMEM, SMEM] + [VMEM] * 5,
        out_specs=(VMEM, VMEM, VMEM),
        name="tokens",
    )(me, source, own, back, resid.reshape(2, HEADS, HEAD), norm_gain.reshape(HEADS, HEAD), meta)
    arrived = exchange(tokens, "z")
    rows = arrived[:, :64].reshape(owners, 2 * D)
    chosen = pl.pallas_call(
        select_kernel,
        out_shape=jax.ShapeDtypeStruct((16, owners, D + HEAD), bf16),
        in_specs=[VMEM, VMEM],
        out_specs=VMEM,
        compiler_params=params(32),
        name="select_rows",
    )(rows, arrived[:, 64])
    chosen = exchange(chosen, XY).reshape(16 * owners, D + HEAD)
    hidden, gates = pl.pallas_call(
        up_kernel,
        out_shape=(
            jax.ShapeDtypeStruct((16, 256, 2 * UNITS), bf16),
            jax.ShapeDtypeStruct((256, HEAD), f32),
        ),
        in_specs=[SMEM] + [VMEM] * 5,
        out_specs=(VMEM, VMEM),
        compiler_params=params(40),
        name="gate_up",
    )(core, chosen, w_gate, w_up, gate_b, up_b)
    hidden = exchange(hidden, XY)
    partial = pl.pallas_call(
        down_kernel,
        out_shape=jax.ShapeDtypeStruct((owners, 2, 16, 2 * HEAD), bf16),
        in_specs=[VMEM] * 4,
        out_specs=VMEM,
        compiler_params=params(40),
        name="down",
    )(hidden, w_down, down_b, gates)
    landed = exchange(partial, "z")
    summed = jnp.sum(landed.astype(f32), axis=0).transpose(1, 0, 2)
    mixture = exchange(summed, XY).reshape(16, 2, 2, HEAD)
    mixture = jnp.where(core[0] == 0, mixture, mixture[:, :, ::-1])
    mixture = mixture.transpose(1, 0, 2, 3).reshape(2, D)
    layer_out = (stream.reshape(2, D) + mixture).astype(bf16)
    return attn.reshape(2, D), layer_out


def solution(mesh):
    fine = Mesh(mesh.devices.reshape(4, 4, 2, 16), ALL)
    rows, experts = P(ALL, None), P(("z", "x", "y", "c"), None)
    cache = P(ALL, None, None)
    placed = (
        rows,
        rows,
        rows,
        P(),
        cache,
        P(ALL),
        cache,
        P(None, "z"),
        P(None, "z"),
        rows,
        rows,
        experts,
        experts,
        P("z", None, PLANE),
    )
    return jax.shard_map(
        on_device, mesh=fine, in_specs=placed, out_specs=(rows, rows), check_vma=False
    )
```

time: 370 us -> 211 us (0.57)
  waiting for transfers between devices: 196 us -> 79.1 us
  between operations: 17 us -> 1.54 us
  matrix products: 15.4 us -> 0 us
  Pallas kernels: 0 us -> 11.1 us
  local copies, waits for them, and re-layouts: 30.8 us -> 22.9 us
  blocking collectives: 70.9 us -> 63.5 us
  starting transfers between devices: 33.7 us -> 29.1 us
    psum x1 -> x0, waiting for transfers between devices: 141 us -> none  [on_device(): hidden = lax.psum(placed.astype(jnp.bfloat16), 'replica')]
    all_to_all x4 -> x5, waiting for transfers between devices: 37.3 us -> 73.2 us  [exchange(): return lax.all_to_all(a, axes, split_axis=0, concat_axis=0, tiled=True)]
    all_gather x1 -> x0, blocking collectives: 23.1 us -> none  [on_device(): lax.all_gather(tags_in, 'replica', axis=0, tiled=True)]
    all_gather x1 -> x0, waiting for transfers between devices: 17.5 us -> none  [on_device(): lax.all_gather(incoming, 'replica', axis=0, tiled=True)]
    unnamed x18 -> x36, local copies, waits for them, and re-layouts: 0.27 us -> 17.7 us
    all_to_all x2, blocking collectives: 47.8 us -> 63.5 us  [exchange(): return lax.all_to_all(a, axes, split_axis=0, concat_axis=0, tiled=True)]
    dot_general x11 -> x0, matrix products: 15.4 us -> none  [the longest x1 6.43 us: on_device(): jnp.einsum('md,fd->mf', tokens, w_gate, preferred_element_type=jnp.float32)]
    reshape x12 -> x2, local copies, waits for them, and re-layouts: 14.8 us -> 0.08 us  [the longest x1 0.04 us: on_device(): mixture = mixture.transpose(1, 0, 2, 3).reshape(2, D)]
  transfers between devices with their start and end apart: 6 -> 8, of which waited for: 5 -> 8; matrix products, arithmetic and copies ran while one was open for 3% -> 2% of each run, Pallas kernels for 0% -> 1%
where the time goes in v1:
time: 211 us; the launch traced here: 210 us
  waiting for transfers between devices  79.1 us (37%)
  blocking collectives  63.5 us (30%)
  starting transfers between devices  29.1 us (14%)
  local copies, waits for them, and re-layouts  22.9 us (11%)
  Pallas kernels  11.1 us (5%)
  other arithmetic  2.3 us (1%)
    all_to_all x5, waiting for transfers between devices, exchange(): return lax.all_to_all(a, axes, split_axis=0, concat_axis=0, tiled=True)  73.2 us
    all_to_all x2, blocking collectives, exchange(): return lax.all_to_all(a, axes, split_axis=0, concat_axis=0, tiled=True)  63.5 us
    all_to_all x5, starting transfers between devices, exchange(): return lax.all_to_all(a, axes, split_axis=0, concat_axis=0, tiled=True)  22.8 us
    unnamed x36, local copies, waits for them, and re-layouts  17.7 us
    ppermute x3, starting transfers between devices, on_device(): swap = lambda a: lax.ppermute(a, 'c', [(0, 1), (1, 0)])  6.25 us
    ppermute x3, waiting for transfers between devices, on_device(): swap = lambda a: lax.ppermute(a, 'c', [(0, 1), (1, 0)])  5.85 us
  transfers between devices with their start and end apart: 8, of which 8 were waited for; matrix products, arithmetic and copies ran while one was open for 2% of the time, Pallas kernels for 1%

profile of v1, /device:TPU:32, one launch (start us, length us, event | category | flops | bytes accessed | tf_op | source)
XLA Modules:
  0.0 209.5 jit_solution(6567895815793298023)
XLA Ops:
  0.6 1.5 slice_reduce_fusion
  2.1 1.3 slice_reduce_fusion.3
  3.4 0.8 broadcast_in_dim.23
  4.2 7.3 %all-to-all-start = ((bf16[32,48,128]{2,1,0:T(8,128)(2,1)}), bf16[32,48,128]{2,1,0:T(8,128)(2,1)S(1)}, u32[]{:S(2)}, u32[]{:S(2)}) async-start(bf16[32,48,128]{2,1,0:T(8,128)(2,1)} %broadcast_in_dim.23), calls=%async_computation | async-start | bytes 786432 | tf_op jit(solution)/shard_map/all_to_all | solution.py:155
  11.6 0.8 broadcast_compare_fusion
  12.4 0.8 select_reduce_fusion
  13.2 8.3 %all-to-all-done.asked_ref = bf16[32,48,128]{2,1,0:T(8,128)(2,1)S(1)} async-done(((bf16[32,48,128]{2,1,0:T(8,128)(2,1)}), bf16[32,48,128]{2,1,0:T(8,128)(2,1)S(1)}, u32[]{:S(2)}, u32[]{:S(2)}) %all-to-all-start) | async-done | bytes 393248 | tf_op jit(solution)/shard_map/all_to_all | solution.py:155
  21.5 0.7 copy-done.11
  22.3 2.7 %guest_attention.1 = bf16[32,32,128]{2,1,0:T(8,128)(2,1)} custom-call(s32[1]{0:T(128)} %bitcast.me_ref, s32[32]{0:T(128)} %bitcast.56, s32[32]{0:T(128)} %bitcast.58, bf16[32,48,128]{2,1,0:T(8,128)(2,1)} %copy-done.11, bf16[256,512]{1,0:T(8,128)(2,1)} %bitcast.42), custom_call_target="tpu_custom_call" | custom-call | tf_op jit(solution)/shard_map/guest_attention/pallas_call | solution.py:205
  25.0 3.9 %all-to-all-start.1 = ((bf16[32,32,128]{2,1,0:T(8,128)(2,1)}), bf16[32,32,128]{2,1,0:T(8,128)(2,1)S(1)}, u32[]{:S(2)}, u32[]{:S(2)}) async-start(bf16[32,32,128]{2,1,0:T(8,128)(2,1)} %guest_attention.1), calls=%async_computation.1 | async-start | bytes 524288 | tf_op jit(solution)/shard_map/all_to_all | solution.py:155
  29.7 0.6 copy.51
  30.3 0.6 pad.9.meta_ref
  30.9 2.1 %resident_attention.1.own_ref = bf16[32,128]{1,0:T(8,128)(2,1)} custom-call(s32[1]{0:T(128)S(6)} %copy.53.len_ref, bf16[32,128]{1,0:T(8,128)(2,1)} %bitcast.47, bf16[4,128]{1,0:T(4,128)(2,1)} %bitcast.54, bf16[128,512]{1,0:T(8,128)(2,1)} %bitcast.44), custom_call_target="tpu_custom_call" | custom-call | tf_op jit(solution)/shard_map/resident_attention/pallas_call | solution.py:197
  33.0 4.8 %all-to-all-done.1.back_ref = bf16[32,32,128]{2,1,0:T(8,128)(2,1)S(1)} async-done(((bf16[32,32,128]{2,1,0:T(8,128)(2,1)}), bf16[32,32,128]{2,1,0:T(8,128)(2,1)S(1)}, u32[]{:S(2)}, u32[]{:S(2)}) %all-to-all-start.1) | async-done | bytes 262176 | tf_op jit(solution)/shard_map/all_to_all | solution.py:155
  37.8 0.7 copy-done.12
  38.5 1.8 tokens.1
  40.3 35.7 %all_to_all.35 = bf16[16,80,128]{2,1,0:T(8,128)(2,1)S(1)} all-to-all(bf16[16,80,128]{2,1,0:T(8,128)(2,1)} %get-tuple-element.9), channel_id=1, replica_groups=mesh['x'=4,'y'=4,'c'=2,'z'=16] {'z'}, dimensions={0} | all-to-all | bytes 655360 | tf_op jit(solution)/shard_map/all_to_all | solution.py:155
  76.0 0.2 copy.49
  76.2 0.2 select_rows.1
  76.5 1.4 copy-done
  77.8 3.7 %all-to-all-start.3 = ((bf16[16,16,4224]{2,1,0:T(8,128)(2,1)}), bf16[16,16,4224]{2,1,0:T(8,128)(2,1)S(1)}, u32[]{:S(2)}, u32[]{:S(2)}) async-start(bf16[16,16,4224]{2,1,0:T(8,128)(2,1)} %copy-done), calls=%async_computation.3 | async-start | bytes 4325376 | tf_op jit(solution)/shard_map/all_to_all | solution.py:155
  81.6 1.9 collective-permute-start
  83.5 2.4 %collective-permute-start.1 = (bf16[192,4096]{1,0:T(8,128)(2,1)}, bf16[192,4096]{1,0:T(8,128)(2,1)S(1)}, u32[]{:S(2)}, u32[]{:S(2)}) collective-permute-start(bf16[192,4096]{1,0:T(8,128)(2,1)} %ua_ref.1), channel_id=1, source_target_pairs={{0,16},{16,0},{1,17},{17,1},{2,18},{18,2},{3,19},{19,3},{4,20},{20... | collective-permute-start | bytes 4718600 | tf_op jit(solution)/shard_map/ppermute | solution.py:189
  85.9 1.2 collective-permute-done.gb_ref
  87.1 1.2 copy-done.4
  88.2 1.1 collective-permute-done.1.ub_ref
  89.3 1.2 copy-done.6
  90.5 21.0 %all-to-all-done.3 = bf16[16,16,4224]{2,1,0:T(8,128)(2,1)S(1)} async-done(((bf16[16,16,4224]{2,1,0:T(8,128)(2,1)}), bf16[16,16,4224]{2,1,0:T(8,128)(2,1)S(1)}, u32[]{:S(2)}, u32[]{:S(2)}) %all-to-all-start.3) | async-done | bytes 2162720 | tf_op jit(solution)/shard_map/all_to_all | solution.py:155
  111.4 1.4 copy-done.2
  112.9 1.4 copy-done.3
  114.3 1.4 copy-done.5
  115.7 1.4 copy-done.7
  117.1 3.0 %gate_up.1 = (bf16[16,256,384]{2,1,0:T(8,128)(2,1)S(1)}, f32[256,128]{1,0:T(8,128)S(1)}) custom-call(s32[1]{0:T(128)} %bitcast.8.core_ref, bf16[256,4224]{1,0:T(8,128)(2,1)S(1)} %bitcast.38, bf16[192,4096]{1,0:T(8,128)(2,1)S(1)} %copy-done.2, bf16[192,4096]{1,0:T(8,128)(2,1)S(1)} %copy-done.3, bf16[192,4096]{1,0:T(8,128)(2,1)S(1)} %copy-done.5, ...), custom_call_target="tpu_custom_call" | custom-call | tf_op jit(solution)/shard_map/gate_up/pallas_call | solution.py:236
  120.1 1.6 copy-done.1
  121.7 4.0 %all-to-all-start.4 = ((bf16[16,256,384]{2,1,0:T(8,128)(2,1)}), bf16[16,256,384]{2,1,0:T(8,128)(2,1)S(1)}, u32[]{:S(2)}, u32[]{:S(2)}) async-start(bf16[16,256,384]{2,1,0:T(8,128)(2,1)} %copy-done.1), calls=%async_computation.4 | async-start | bytes 6291456 | tf_op jit(solution)/shard_map/all_to_all | solution.py:155
  125.7 1.9 collective-permute-start.2
  127.7 3.6 %collective-permute-done.2.wb_ref = bf16[4,1536,128]{2,1,0:T(8,128)(2,1)S(1)} collective-permute-done((bf16[4,1536,128]{2,1,0:T(8,128)(2,1)}, bf16[4,1536,128]{2,1,0:T(8,128)(2,1)S(1)}, u32[]{:S(2)}, u32[]{:S(2)}) %collective-permute-start.2) | collective-permute-done | bytes 1572896 | tf_op jit(solution)/shard_map/ppermute | solution.py:189
  131.3 1.2 copy-done.9
  132.4 32.1 %all-to-all-done.4.act_ref = bf16[16,256,384]{2,1,0:T(8,128)(2,1)S(1)} async-done(((bf16[16,256,384]{2,1,0:T(8,128)(2,1)}), bf16[16,256,384]{2,1,0:T(8,128)(2,1)S(1)}, u32[]{:S(2)}, u32[]{:S(2)}) %all-to-all-start.4) | async-done | bytes 3145760 | tf_op jit(solution)/shard_map/all_to_all | solution.py:155
  164.5 1.4 copy-done.8
  165.9 1.4 copy-done.10
  167.3 1.3 down.1
  168.6 27.8 %all_to_all.36 = bf16[16,2,16,256]{3,2,1,0:T(8,128)(2,1)S(1)} all-to-all(bf16[16,2,16,256]{3,2,1,0:T(8,128)(2,1)S(1)} %down.1), channel_id=1, replica_groups=mesh['x'=4,'y'=4,'c'=2,'z'=16] {'z'}, dimensions={0} | all-to-all | bytes 524288 | tf_op jit(solution)/shard_map/all_to_all | solution.py:155
  196.5 0.6 copy.35
  197.1 3.9 %all-to-all-start.6 = ((f32[16,2,256]{2,1,0:T(2,128)}), f32[16,2,256]{2,1,0:T(2,128)S(1)}, u32[]{:S(2)}, u32[]{:S(2)}) async-start(f32[16,2,256]{2,1,0:T(2,128)} %copy.35), calls=%async_computation.6 | async-start | bytes 65536 | tf_op jit(solution)/shard_map/all_to_all | solution.py:155
  201.0 0.6 copy.50
  201.7 7.0 %all-to-all-done.6 = f32[16,2,256]{2,1,0:T(2,128)S(1)} async-done(((f32[16,2,256]{2,1,0:T(2,128)}), f32[16,2,256]{2,1,0:T(2,128)S(1)}, u32[]{:S(2)}, u32[]{:S(2)}) %all-to-all-start.6) | async-done | bytes 32800 | tf_op jit(solution)/shard_map/all_to_all | solution.py:155
  208.9 0.6 fusion
  (35 shorter events, 0.4 us)
Async XLA Ops:
  0.6 29.0 %copy-start.14 = (bf16[2,4096]{1,0:T(2,128)(2,1)S(1)}, bf16[2,4096]{1,0:T(2,128)(2,1)}, u32[]{:S(2)}) copy-start(bf16[2,4096]{1,0:T(2,128)(2,1)} %param.16) | copy-start | bytes 49156
  4.2 17.3 %all-to-all-start = ((bf16[32,48,128]{2,1,0:T(8,128)(2,1)}), bf16[32,48,128]{2,1,0:T(8,128)(2,1)S(1)}, u32[]{:S(2)}, u32[]{:S(2)}) async-start(bf16[32,48,128]{2,1,0:T(8,128)(2,1)} %broadcast_in_dim.23), calls=%async_computation | async-start | bytes 786432 | tf_op jit(solution)/shard_map/all_to_all | solution.py:155
  21.5 0.7 copy-start.11
  25.0 12.8 %all-to-all-start.1 = ((bf16[32,32,128]{2,1,0:T(8,128)(2,1)}), bf16[32,32,128]{2,1,0:T(8,128)(2,1)S(1)}, u32[]{:S(2)}, u32[]{:S(2)}) async-start(bf16[32,32,128]{2,1,0:T(8,128)(2,1)} %guest_attention.1), calls=%async_computation.1 | async-start | bytes 524288 | tf_op jit(solution)/shard_map/all_to_all | solution.py:155
  37.8 0.7 copy-start.12
  76.5 1.4 copy-start
  77.8 33.6 %all-to-all-start.3 = ((bf16[16,16,4224]{2,1,0:T(8,128)(2,1)}), bf16[16,16,4224]{2,1,0:T(8,128)(2,1)S(1)}, u32[]{:S(2)}, u32[]{:S(2)}) async-start(bf16[16,16,4224]{2,1,0:T(8,128)(2,1)} %copy-done), calls=%async_computation.3 | async-start | bytes 4325376 | tf_op jit(solution)/shard_map/all_to_all | solution.py:155
  81.6 5.5 %collective-permute-start = (bf16[192,4096]{1,0:T(8,128)(2,1)}, bf16[192,4096]{1,0:T(8,128)(2,1)S(1)}, u32[]{:S(2)}, u32[]{:S(2)}) collective-permute-start(bf16[192,4096]{1,0:T(8,128)(2,1)} %ga_ref.1), channel_id=1, source_target_pairs={{0,16},{16,0},{1,17},{17,1},{2,18},{18,2},{3,19},{19,3},{4,20},{20... | collective-permute-start | bytes 4718600 | tf_op jit(solution)/shard_map/ppermute | solution.py:189
  83.5 5.8 %collective-permute-start.1 = (bf16[192,4096]{1,0:T(8,128)(2,1)}, bf16[192,4096]{1,0:T(8,128)(2,1)S(1)}, u32[]{:S(2)}, u32[]{:S(2)}) collective-permute-start(bf16[192,4096]{1,0:T(8,128)(2,1)} %ua_ref.1), channel_id=1, source_target_pairs={{0,16},{16,0},{1,17},{17,1},{2,18},{18,2},{3,19},{19,3},{4,20},{20... | collective-permute-start | bytes 4718600 | tf_op jit(solution)/shard_map/ppermute | solution.py:189
  87.1 1.2 copy-start.4
  89.3 1.2 copy-start.6
  111.4 1.4 copy-start.2
  112.9 1.4 copy-start.3
  114.3 1.4 copy-start.5
  115.7 1.4 copy-start.7
  120.1 1.6 copy-start.1
  121.7 42.8 %all-to-all-start.4 = ((bf16[16,256,384]{2,1,0:T(8,128)(2,1)}), bf16[16,256,384]{2,1,0:T(8,128)(2,1)S(1)}, u32[]{:S(2)}, u32[]{:S(2)}) async-start(bf16[16,256,384]{2,1,0:T(8,128)(2,1)} %copy-done.1), calls=%async_computation.4 | async-start | bytes 6291456 | tf_op jit(solution)/shard_map/all_to_all | solution.py:155
  125.7 5.5 %collective-permute-start.2 = (bf16[4,1536,128]{2,1,0:T(8,128)(2,1)}, bf16[4,1536,128]{2,1,0:T(8,128)(2,1)S(1)}, u32[]{:S(2)}, u32[]{:S(2)}) collective-permute-start(bf16[4,1536,128]{2,1,0:T(8,128)(2,1)} %wa_ref.1), channel_id=1, source_target_pairs={{0,16},{16,0},{1,17},{17,1},{2,18},{18,2},{3,19},{19,3},{4,20},{20... | collective-permute-start | bytes 4718600 | tf_op jit(solution)/shard_map/ppermute | solution.py:189
  131.3 1.2 copy-start.9
  164.5 1.4 copy-start.8
  165.9 1.4 copy-start.10
  167.3 33.7 %copy-start.15 = (bf16[2,32,128]{2,1,0:T(8,128)(2,1)S(1)}, bf16[2,32,128]{2,1,0:T(8,128)(2,1)}, u32[]{:S(2)}) copy-start(bf16[2,32,128]{2,1,0:T(8,128)(2,1)} %get-tuple-element.7) | copy-start | bytes 49156
  167.3 41.5 %copy-start.13 = (f32[2,32,128]{2,1,0:T(8,128)S(1)}, f32[2,32,128]{2,1,0:T(8,128)}, u32[]{:S(2)}) copy-start(f32[2,32,128]{2,1,0:T(8,128)} %get-tuple-element.8) | copy-start | bytes 98308
  197.1 11.5 %all-to-all-start.6 = ((f32[16,2,256]{2,1,0:T(2,128)}), f32[16,2,256]{2,1,0:T(2,128)S(1)}, u32[]{:S(2)}, u32[]{:S(2)}) async-start(f32[16,2,256]{2,1,0:T(2,128)} %copy.35), calls=%async_computation.6 | async-start | bytes 65536 | tf_op jit(solution)/shard_map/all_to_all | solution.py:155

commit v2 on v1

v2 whole, which is shorter than its diff:
```python
import functools
import math

import jax
import jax.numpy as jnp
from jax import lax
from jax.experimental import pallas as pl
from jax.experimental.pallas import tpu as pltpu
from jax.sharding import Mesh
from jax.sharding import PartitionSpec as P

HEADS = 32
GROUP = 16
HEAD = 128
D = 4096
FFW = 1536
LOCAL = 4
UNITS = 192
X = ("xh", "xl")
Y = ("yh", "yl")
XY = X + Y
PLANE = XY + ("c",)
Z = ("zh", "zl")
ALL = PLANE + Z
VMEM = pl.BlockSpec(memory_space=pltpu.VMEM)
SMEM = pl.BlockSpec(memory_space=pltpu.SMEM)
HBM = pl.BlockSpec(memory_space=pltpu.HBM)


def params(mib):
    return pltpu.CompilerParams(vmem_limit_bytes=mib << 20)


def attend(q, cache_ref, fresh, length):
    slots = cache_ref.shape[0]
    fresh = fresh.astype(jnp.float32)
    outs = []
    for g in range(2):
        qg = q[g * GROUP : (g + 1) * GROUP]
        keys = cache_ref[:, g * HEAD : (g + 1) * HEAD]
        values = cache_ref[:, (2 + g) * HEAD : (3 + g) * HEAD]
        scale = 1.0 / math.sqrt(HEAD)
        scores = lax.dot_general(
            qg, keys, (((1,), (1,)), ((), ())), preferred_element_type=jnp.float32
        )
        scores = scores * scale
        live = lax.broadcasted_iota(jnp.int32, (GROUP, slots), 1) < length
        scores = jnp.where(live, scores, -1e30)
        last = (
            jnp.sum(qg.astype(jnp.float32) * fresh[g : g + 1], axis=1, keepdims=True)
            * scale
        )
        peak = jnp.maximum(jnp.max(scores, axis=1, keepdims=True), last)
        weights = jnp.where(live, jnp.exp(scores - peak), 0.0).astype(jnp.bfloat16)
        end = jnp.exp(last - peak).astype(jnp.bfloat16).astype(jnp.float32)
        total = jnp.sum(weights.astype(jnp.float32), axis=1, keepdims=True) + end
        summed = jnp.dot(weights, values, preferred_element_type=jnp.float32)
        summed = summed + end * fresh[2 + g : 3 + g]
        outs.append(summed / total)
    return jnp.concatenate(outs, axis=0)


def ask_kernel(q_ref, kv_ref, ask_ref, own_ref, line_ref):
    q = q_ref[...].astype(jnp.float32)
    kv = kv_ref[...].astype(jnp.float32)
    line_ref[...] = jnp.zeros(line_ref.shape, jnp.float32)
    for r in range(2):
        for h in range(HEADS):
            line_ref[r, h : h + 1] = q[r : r + 1, h * HEAD : (h + 1) * HEAD]
        for h in range(4):
            line_ref[r, 32 + h : 33 + h] = kv[r : r + 1, h * HEAD : (h + 1) * HEAD]
    own_ref[...] = line_ref[0].astype(jnp.bfloat16)
    ask = line_ref[1].astype(jnp.bfloat16)
    for p in range(ask_ref.shape[0]):
        ask_ref[p] = ask


def resident_kernel(len_ref, own_ref, cache_ref, out_ref):
    own = own_ref[...]
    out = attend(own[:32], cache_ref, own[32:48][:4], len_ref[0])
    out_ref[...] = out.astype(jnp.bfloat16)


def guest_kernel(me_ref, from_ref, len_ref, asked_ref, cache_ref, out_ref):
    me = me_ref[0]

    def look(i, found):
        return jnp.where(from_ref[i] == me, i, found)

    target = lax.fori_loop(0, from_ref.shape[0], look, 0)
    asked = asked_ref[target]
    out = attend(asked[:32], cache_ref, asked[32:48][:4], len_ref[me])
    out = out.astype(jnp.bfloat16)
    for r in range(out_ref.shape[0]):
        out_ref[r] = out


def token_kernel(
    me_ref, from_ref, own_ref, back_ref, resid_ref, gain_ref, meta_ref, attn_ref, stream_ref, out_ref
):
    root = from_ref[me_ref[0]]
    rows = (own_ref[...], back_ref[root])
    for r in range(2):
        attn_ref[r] = rows[r]
        stream = resid_ref[r].astype(jnp.float32) + rows[r].astype(jnp.float32)
        stream_ref[r] = stream
        square = jnp.sum(jnp.sum(stream * stream, axis=1, keepdims=True), axis=0, keepdims=True)
        normed = (stream * lax.rsqrt(square / D + 1e-06) * gain_ref[...]).astype(jnp.bfloat16)
        for e in range(out_ref.shape[0]):
            out_ref[e, r * 32 : (r + 1) * 32] = normed
    for e in range(out_ref.shape[0]):
        out_ref[e, 64:80] = meta_ref[...]


def select_kernel(expert_ref, rows_ref, meta_ref, out_ref):
    meta = meta_ref[...].astype(jnp.float32)
    mine = lax.broadcasted_iota(jnp.int32, meta.shape, 1) == expert_ref[0]
    meta = jnp.sum(jnp.where(mine, meta, 0.0), axis=1)
    line = meta.astype(jnp.bfloat16)
    first = rows_ref[:, :D].astype(jnp.float32)
    second = rows_ref[:, D:].astype(jnp.float32)
    for x in range(LOCAL):
        pick = meta[:, 16 + x : 17 + x] > 0.5
        row = jnp.where(pick, second, first).astype(jnp.bfloat16)
        for y in range(4):
            out_ref[x * 4 + y, :, :D] = row
            out_ref[x * 4 + y, :, D:] = line


def up_kernel(
    core_ref, rows_ref, ga_ref, ua_ref, gb_ref, ub_ref, out_ref, gate_ref, held_ref, sems
):
    copies = [
        pltpu.make_async_copy(w_ref, held_ref.at[pl.ds(i * UNITS, UNITS)], sems.at[i])
        for i, w_ref in enumerate((ga_ref, ua_ref, gb_ref, ub_ref))
    ]
    for copy in copies:
        copy.start()
    for copy in copies:
        copy.wait()
    dims = (((1,), (1,)), ((), ()))
    total = lax.dot_general(
        rows_ref[:, :D], held_ref[...], dims, preferred_element_type=jnp.float32
    )
    parts = [total[:, i * UNITS : (i + 1) * UNITS] for i in range(4)]
    acts = [
        gate * (1.0 / (1.0 + jnp.exp(-gate))) * up
        for gate, up in (parts[:2], parts[2:])
    ]
    both = jnp.where(
        core_ref[0] == 0,
        jnp.concatenate(acts, axis=1),
        jnp.concatenate(acts[::-1], axis=1),
    ).astype(jnp.bfloat16)
    for x in range(4):
        for y in range(4):
            there = slice((x * 4 + y) * 16, (x * 4 + y + 1) * 16)
            here = slice((x // 2 * 2 + y // 2) * 16, (x // 2 * 2 + y // 2 + 1) * 16)
            gate_ref[x % 2 * 2 + y % 2, here] = rows_ref[there, D:]
            for to_x in (x % 2, x % 2 + 2):
                for to_y in (y % 2, y % 2 + 2):
                    out_ref[to_x * 4 + to_y, here] = both[there]


def down_kernel(place_ref, act_ref, gate_ref, *refs):
    w_refs, (out_ref, held_ref, sems) = refs[:10], refs[10:]
    copies = []
    for x in range(LOCAL):
        sources = []
        for c in range(2):
            own, by_x, by_both, *by_y = w_refs[5 * c : 5 * c + 5]
            sources += [own.at[x], by_x.at[x], by_y[x // 2].at[x % 2], by_both.at[x]]
        copies.append(
            [
                pltpu.make_async_copy(source, held_ref.at[x, i], sems.at[x, i])
                for i, source in enumerate(sources)
            ]
        )
        for copy in copies[-1]:
            copy.start()
    n = act_ref.shape[1]
    row = lax.broadcasted_iota(jnp.int32, (2 * n, n), 0)
    slot = lax.broadcasted_iota(jnp.int32, (2 * n, n), 1)
    twice = jnp.where(row // 2 == slot, 1.0, 0.0).astype(jnp.bfloat16)
    gates = gate_ref[place_ref[0] * 2 + place_ref[1]]
    gates = jnp.dot(twice, gates, preferred_element_type=jnp.float32)
    lane = lax.broadcasted_iota(jnp.int32, gates.shape, 1)
    second = lax.broadcasted_iota(jnp.int32, gates.shape, 0) % 2
    sums = [0.0] * 4
    for x in range(LOCAL):
        act = jnp.concatenate([act_ref[x * 4 + y] for y in range(4)], axis=1)
        act = jnp.dot(twice, act, preferred_element_type=jnp.float32).astype(jnp.bfloat16)
        at = second * LOCAL + x
        weight = jnp.sum(
            jnp.where((lane == at) | (lane == at + 8), gates, 0.0), axis=1, keepdims=True
        )
        for copy in copies[x]:
            copy.wait()
        for b in range(4):
            w = jnp.concatenate([held_ref[x, 2 * b], held_ref[x, 2 * b + 1]], axis=1)
            sums[b] += weight * jnp.dot(act, w, preferred_element_type=jnp.float32)
    for p in range(out_ref.shape[0]):
        for b in range(4):
            part = sums[b][p * 2 : (p + 1) * 2].astype(jnp.bfloat16)
            out_ref[p, :, b * 256 : (b + 1) * 256] = part


def last_kernel(place_ref, landed_ref, stream_ref, out_ref):
    core = place_ref[2]
    for g in range(4):
        total = landed_ref[g * 16].astype(jnp.float32)
        for z in range(1, 16):
            total += landed_ref[g * 16 + z].astype(jnp.float32)
        for b in range(8):
            of = core if b < 4 else 1 - core
            x = (g // 2) * 2 + place_ref[0]
            y = (g % 2) * 2 + place_ref[1]
            if b & 1:
                x = lax.rem(x + 1 + 2 * of, 4)
            if b & 2:
                y = lax.rem(y + 1 + 2 * of, 4)
            at = pl.ds(pl.multiple_of(x * 1024 + y * 256 + of * HEAD, HEAD), HEAD)
            mixture = total[:, b * HEAD : (b + 1) * HEAD]
            out_ref[:, at] = (stream_ref[:, at] + mixture).astype(jnp.bfloat16)


def in_hbm(a):
    return pltpu.with_memory_space_constraint(a, pltpu.HBM)


def tie(first, a):
    return lax.optimization_barrier((first, a))[1]


def exchange(a, axes):
    return lax.all_to_all(a, axes, split_axis=0, concat_axis=0, tiled=True)


def pick_table(expert_ids, gate_wts, owners):
    wanted = jnp.arange(owners * LOCAL).reshape(owners, 1, LOCAL, 1)
    hit = expert_ids[None, :, None, :] == wanted
    gates = jnp.sum(jnp.where(hit, gate_wts[None, :, None, :], 0.0), axis=-1)
    high = gates.astype(jnp.bfloat16)
    rest = (gates - high.astype(jnp.float32)).astype(jnp.bfloat16)
    second = jnp.any(hit[:, 1], axis=-1).astype(jnp.bfloat16)
    line = jnp.concatenate([high.reshape(owners, 8), rest.reshape(owners, 8), second], axis=1)
    return jnp.pad(line, ((0, 0), (0, 108)))


def on_device(
    queries,
    fresh_key_value,
    resid,
    norm_gain,
    res_cache,
    res_len,
    long_cache,
    long_len,
    migrate_from,
    expert_ids,
    gate_wts,
    w_gate,
    w_up,
    w_down,
):
    bf16, f32 = jnp.bfloat16, jnp.float32
    core = lax.axis_index("c").reshape(1)
    place = jnp.stack([lax.axis_index(a) for a in ("xl", "yl", "c")])
    expert = lax.axis_index(Z).reshape(1)
    me = lax.axis_index(PLANE).reshape(1)
    owners = 16
    swap = lambda a: lax.ppermute(a, "c", [(0, 1), (1, 0)])

    ask, mine = pl.pallas_call(
        ask_kernel,
        out_shape=(
            jax.ShapeDtypeStruct((32, 48, HEAD), bf16),
            jax.ShapeDtypeStruct((48, HEAD), bf16),
        ),
        in_specs=[VMEM, VMEM],
        out_specs=(VMEM, VMEM),
        scratch_shapes=[pltpu.VMEM((2, 48, HEAD), f32)],
        compiler_params=params(4),
        name="ask",
    )(in_hbm(queries), in_hbm(fresh_key_value))
    asked = exchange(ask, PLANE)

    own = pl.pallas_call(
        resident_kernel,
        out_shape=jax.ShapeDtypeStruct((HEADS, HEAD), bf16),
        in_specs=[SMEM, VMEM, VMEM],
        out_specs=VMEM,
        compiler_params=params(4),
        name="resident_attention",
    )(res_len, mine, res_cache[0])
    onward = [(i * 2 + c, ((i + 3 + 2 * c) % 4) * 2 + c) for i in range(4) for c in range(2)]
    far = [
        (i * 8 + t, (onward[2 * i + t % 2][1] // 2) * 8 + u) for i in range(4) for t, u in onward
    ]
    source = migrate_from.reshape(32)
    guest = pl.pallas_call(
        guest_kernel,
        out_shape=jax.ShapeDtypeStruct((32, HEADS, HEAD), bf16),
        in_specs=[SMEM, SMEM, SMEM, VMEM, VMEM],
        out_specs=VMEM,
        compiler_params=params(8),
        name="guest_attention",
    )(me, in_hbm(source), in_hbm(long_len.reshape(32)), asked, in_hbm(long_cache[0]))
    back = exchange(guest, PLANE)
    meta = pick_table(expert_ids, gate_wts, owners)
    attn, stream, tokens = pl.pallas_call(
        token_kernel,
        out_shape=(
            jax.ShapeDtypeStruct((2, HEADS, HEAD), bf16),
            jax.ShapeDtypeStruct((2, HEADS, HEAD), f32),
            jax.ShapeDtypeStruct((owners, 80, HEAD), bf16),
        ),
        in_specs=[SMEM, SMEM] + [VMEM] * 5,
        out_specs=(VMEM, VMEM, VMEM),
        compiler_params=params(8),
        name="tokens",
    )(me, source, own, back, resid.reshape(2, HEADS, HEAD), norm_gain.reshape(HEADS, HEAD), meta)
    later = tie(stream, w_down)
    by_both = lax.ppermute(later, PLANE, far)
    by_x = lax.ppermute(later, X + ("c",), onward)
    by_y = [lax.ppermute(a, Y + ("c",), onward) for a in (later[:2], later[2:])]

    arrived = exchange(tokens, ("zl", "zh"))
    chosen = pl.pallas_call(
        select_kernel,
        out_shape=jax.ShapeDtypeStruct((16, owners, D + HEAD), bf16),
        in_specs=[SMEM, VMEM, VMEM],
        out_specs=VMEM,
        compiler_params=params(12),
        name="select_rows",
    )(expert, arrived[:, :64].reshape(owners, 2 * D), arrived[:, 64:])
    chosen, by_both, by_x, by_y = lax.optimization_barrier((chosen, by_both, by_x, by_y))
    gate_b, up_b = swap(w_gate), swap(w_up)
    downs = [w_down, by_x, by_both] + by_y
    downs += [swap(a) for a in downs]
    chosen = exchange(chosen, XY).reshape(16 * owners, D + HEAD)
    hidden, gates = pl.pallas_call(
        up_kernel,
        out_shape=(
            jax.ShapeDtypeStruct((16, 64, 2 * UNITS), bf16),
            jax.ShapeDtypeStruct((4, 64, HEAD), bf16),
        ),
        in_specs=[SMEM, VMEM] + [HBM] * 4,
        out_specs=(VMEM, VMEM),
        scratch_shapes=[pltpu.VMEM((4 * UNITS, D), bf16), pltpu.SemaphoreType.DMA((4,))],
        compiler_params=params(20),
        name="gate_up",
    )(core, chosen, *[in_hbm(a) for a in (w_gate, w_up, gate_b, up_b)])
    hidden = exchange(hidden, XY)
    partial = pl.pallas_call(
        down_kernel,
        out_shape=jax.ShapeDtypeStruct((64, 2, 8 * HEAD), bf16),
        in_specs=[SMEM, VMEM, VMEM] + [HBM] * 10,
        out_specs=VMEM,
        scratch_shapes=[
            pltpu.VMEM((LOCAL, 8, FFW, HEAD), bf16),
            pltpu.SemaphoreType.DMA((LOCAL, 8)),
        ],
        compiler_params=params(24),
        name="down",
    )(place, hidden, gates, *[in_hbm(a) for a in downs])
    landed = exchange(partial, ("xh", "yh", "zl", "zh"))
    layer_out = pl.pallas_call(
        last_kernel,
        out_shape=jax.ShapeDtypeStruct((2, D), bf16),
        in_specs=[SMEM, VMEM, VMEM],
        out_specs=VMEM,
        compiler_params=params(4),
        name="layer_out",
    )(place, landed, stream.reshape(2, D))
    return attn.reshape(2, D), layer_out


def solution(mesh):
    fine = Mesh(mesh.devices.reshape(2, 2, 2, 2, 2, 4, 4), ALL)
    rows, experts = P(ALL, None), P(Z + PLANE, None)
    cache = P(ALL, None, None)
    placed = (
        rows,
        rows,
        rows,
        P(),
        cache,
        P(ALL),
        cache,
        P(None, Z),
        P(None, Z),
        rows,
        rows,
        experts,
        experts,
        P(Z, None, PLANE),
    )
    return jax.shard_map(
        on_device, mesh=fine, in_specs=placed, out_specs=(rows, rows), check_vma=False
    )
```

time: 211 us -> 184 us (0.87)
  blocking collectives: 63.5 us -> 0 us
  starting transfers between devices: 29.1 us -> 75.3 us
  local copies, waits for them, and re-layouts: 22.9 us -> 6.42 us
  Pallas kernels: 11.1 us -> 21.6 us
  waiting for transfers between devices: 79.1 us -> 76.2 us
    all_to_all x2 -> x0, blocking collectives: 63.5 us -> none  [exchange(): return lax.all_to_all(a, axes, split_axis=0, concat_axis=0, tiled=True)]
    all_to_all x5 -> x6, starting transfers between devices: 22.8 us -> 48.4 us  [exchange(): return lax.all_to_all(a, axes, split_axis=0, concat_axis=0, tiled=True)]
    unnamed x36 -> x20, local copies, waits for them, and re-layouts: 17.7 us -> 4.86 us
    ppermute x0 -> x4, starting transfers between devices: none -> 12 us  [the longest x2 5.54 us: on_device(): by_y = [lax.ppermute(a, Y + ('c',), onward) for a in (later[:2], later[2:])]]
    pallas_call x2 -> x4, Pallas kernels: 4.28 us -> 15.4 us  [the longest x1 6.74 us: on_device(): pl.pallas_call(down_kernel, out_shape=jax.ShapeDtypeStruct((64, 2, 8 * HE...]
    ppermute x3 -> x7, starting transfers between devices: 6.25 us -> 14.9 us  [on_device(): swap = lambda a: lax.ppermute(a, 'c', [(0, 1), (1, 0)])]
    ppermute x3 -> x7, waiting for transfers between devices: 5.85 us -> 0.02 us  [on_device(): swap = lambda a: lax.ppermute(a, 'c', [(0, 1), (1, 0)])]
    all_to_all x5 -> x6, waiting for transfers between devices: 73.2 us -> 75.2 us  [exchange(): return lax.all_to_all(a, axes, split_axis=0, concat_axis=0, tiled=True)]
  transfers between devices with their start and end apart: 8 -> 17, of which waited for: 8 -> 7; matrix products, arithmetic and copies ran while one was open for 2% -> 3% of each run, Pallas kernels for 1% -> 4%
where the time goes in v2:
time: 184 us; the launch traced here: 183 us
  waiting for transfers between devices  76.2 us (41%)
  starting transfers between devices  75.3 us (41%)
  Pallas kernels  21.6 us (12%)
  local copies, waits for them, and re-layouts  6.42 us (3%)
    all_to_all x6, waiting for transfers between devices, exchange(): return lax.all_to_all(a, axes, split_axis=0, concat_axis=0, tiled=True)  75.2 us
    all_to_all x6, starting transfers between devices, exchange(): return lax.all_to_all(a, axes, split_axis=0, concat_axis=0, tiled=True)  48.4 us
    ppermute x7, starting transfers between devices, on_device(): swap = lambda a: lax.ppermute(a, 'c', [(0, 1), (1, 0)])  14.9 us
    pallas_call x1, Pallas kernels, on_device(): pl.pallas_call(down_kernel, out_shape=jax.ShapeDtypeStruct((64, 2, 8 * HE...  6.74 us
    pallas_call x1, Pallas kernels, on_device(): pl.pallas_call(up_kernel, out_shape=(jax.ShapeDtypeStruct((16, 64, 2 * UN...  5.88 us
    ppermute x2, starting transfers between devices, on_device(): by_y = [lax.ppermute(a, Y + ('c',), onward) for a in (later[:2], later[2:])]  5.54 us
    unnamed x20, local copies, waits for them, and re-layouts  4.86 us
  transfers between devices with their start and end apart: 17, of which 7 were waited for; matrix products, arithmetic and copies ran while one was open for 3% of the time, Pallas kernels for 4%

profile of v2, /device:TPU:32, one launch (start us, length us, event | category | flops | bytes accessed | tf_op | source)
XLA Modules:
  0.0 182.8 jit_solution(9972739612019853099)
XLA Ops:
  0.6 0.0 copy-start.2
  0.7 1.5 ask.1
  2.2 7.3 %all-to-all-start = ((bf16[32,48,128]{2,1,0:T(8,128)(2,1)}), bf16[32,48,128]{2,1,0:T(8,128)(2,1)S(1)}, u32[]{:S(2)}, u32[]{:S(2)}) async-start(bf16[32,48,128]{2,1,0:T(8,128)(2,1)} %get-tuple-element.16), calls=%async_computation | async-start | bytes 786432 | tf_op jit(solution)/shard_map/all_to_all | solution.py:236
  9.5 0.8 select_reduce_fusion
  10.3 0.1 copy.22
  11.1 0.7 copy.36
  11.8 0.8 broadcast_compare_fusion
  12.6 0.1 copy.24
  12.7 0.1 copy.23
  12.7 0.9 copy-done
  13.7 0.6 resident_attention.1.own_ref
  14.2 5.2 %all-to-all-done.asked_ref = bf16[32,48,128]{2,1,0:T(8,128)(2,1)S(1)} async-done(((bf16[32,48,128]{2,1,0:T(8,128)(2,1)}), bf16[32,48,128]{2,1,0:T(8,128)(2,1)S(1)}, u32[]{:S(2)}, u32[]{:S(2)}) %all-to-all-start) | async-done | bytes 393248 | tf_op jit(solution)/shard_map/all_to_all | solution.py:236
  19.5 2.6 %guest_attention.1 = bf16[32,32,128]{2,1,0:T(8,128)(2,1)} custom-call(s32[1]{0:T(128)} %bitcast.me_ref, s32[32]{0:T(128)} %bitcast.36, s32[32]{0:T(128)} %bitcast.44, bf16[32,48,128]{2,1,0:T(8,128)(2,1)S(1)} %all-to-all-done.asked_ref, bf16[256,512]{1,0:T(8,128)(2,1)} %bitcast.39), custom_call_target="tpu_custom_call" | custom-call | tf_op jit(solution)/shard_map/guest_attention/pallas_call | solution.py:301
  22.1 3.9 %all-to-all-start.1 = ((bf16[32,32,128]{2,1,0:T(8,128)(2,1)}), bf16[32,32,128]{2,1,0:T(8,128)(2,1)S(1)}, u32[]{:S(2)}, u32[]{:S(2)}) async-start(bf16[32,32,128]{2,1,0:T(8,128)(2,1)} %guest_attention.1), calls=%async_computation.1 | async-start | bytes 524288 | tf_op jit(solution)/shard_map/all_to_all | solution.py:236
  26.0 0.1 fusion.4.meta_ref
  26.1 8.8 %all-to-all-done.1.back_ref = bf16[32,32,128]{2,1,0:T(8,128)(2,1)S(1)} async-done(((bf16[32,32,128]{2,1,0:T(8,128)(2,1)}), bf16[32,32,128]{2,1,0:T(8,128)(2,1)S(1)}, u32[]{:S(2)}, u32[]{:S(2)}) %all-to-all-start.1) | async-done | bytes 262176 | tf_op jit(solution)/shard_map/all_to_all | solution.py:236
  34.9 1.4 tokens.1
  36.3 3.6 %collective-permute-start = (bf16[4,1536,128]{2,1,0:T(8,128)(2,1)S(1)}, bf16[4,1536,128]{2,1,0:T(8,128)(2,1)S(1)}, u32[]{:S(2)}, u32[]{:S(2)}) collective-permute-start(bf16[4,1536,128]{2,1,0:T(8,128)(2,1)S(1)} %copy-done.3), channel_id=1, source_target_pairs={{0,480},{16,176},{32,384},{48,208},{64,416},{80,240},{96,448},{112... | collective-permute-start | bytes 4718600 | tf_op jit(solution)/shard_map/ppermute | solution.py:324
  39.9 2.8 %collective-permute-start.1 = (bf16[4,1536,128]{2,1,0:T(8,128)(2,1)S(1)}, bf16[4,1536,128]{2,1,0:T(8,128)(2,1)}, u32[]{:S(2)}, u32[]{:S(2)}) collective-permute-start(bf16[4,1536,128]{2,1,0:T(8,128)(2,1)S(1)} %copy-done.3), channel_id=1, source_target_pairs={{0,384},{16,144},{128,0},{144,272},{256,128},{272,400},{384,256},{... | collective-permute-start | bytes 4718600 | tf_op jit(solution)/shard_map/ppermute | solution.py:325
  42.7 15.2 %all-to-all-start.2 = ((bf16[16,80,128]{2,1,0:T(8,128)(2,1)}), bf16[16,80,128]{2,1,0:T(8,128)(2,1)S(1)}, u32[]{:S(2)}, u32[]{:S(2)}) async-start(bf16[16,80,128]{2,1,0:T(8,128)(2,1)} %get-tuple-element.18), calls=%async_computation.2 | async-start | bytes 655360 | tf_op jit(solution)/shard_map/all_to_all | solution.py:236
  58.0 1.3 fusion.5
  59.2 2.3 %collective-permute-start.2 = (bf16[2,1536,128]{2,1,0:T(8,128)(2,1)}, bf16[2,1536,128]{2,1,0:T(8,128)(2,1)}, u32[]{:S(2)}, u32[]{:S(2)}) collective-permute-start(bf16[2,1536,128]{2,1,0:T(8,128)(2,1)} %get-tuple-element.29), channel_id=1, source_target_pairs={{0,96},{16,48},{32,0},{48,80},{64,32},{80,112},{96,64},{112,16},{1... | collective-permute-start | bytes 2359304 | tf_op jit(solution)/shard_map/ppermute | solution.py:326
  61.5 3.3 %collective-permute-start.3 = (bf16[2,1536,128]{2,1,0:T(8,128)(2,1)}, bf16[2,1536,128]{2,1,0:T(8,128)(2,1)}, u32[]{:S(2)}, u32[]{:S(2)}) collective-permute-start(bf16[2,1536,128]{2,1,0:T(8,128)(2,1)} %get-tuple-element.28), channel_id=1, source_target_pairs={{0,96},{16,48},{32,0},{48,80},{64,32},{80,112},{96,64},{112,16},{1... | collective-permute-start | bytes 2359304 | tf_op jit(solution)/shard_map/ppermute | solution.py:326
  64.8 14.2 %all-to-all-done.2 = bf16[16,80,128]{2,1,0:T(8,128)(2,1)S(1)} async-done(((bf16[16,80,128]{2,1,0:T(8,128)(2,1)}), bf16[16,80,128]{2,1,0:T(8,128)(2,1)S(1)}, u32[]{:S(2)}, u32[]{:S(2)}) %all-to-all-start.2) | async-done | bytes 327712 | tf_op jit(solution)/shard_map/all_to_all | solution.py:236
  79.0 0.2 copy.33
  79.2 1.6 select_rows.1
  80.9 1.0 collective-permute-done.3.refs_4_
  81.9 0.0 collective-permute-done.1.refs_1_
  81.9 1.2 copy-done.6
  83.0 4.7 %all-to-all-start.3 = ((bf16[16,16,4224]{2,1,0:T(8,128)(2,1)}), bf16[16,16,4224]{2,1,0:T(8,128)(2,1)S(1)}, u32[]{:S(2)}, u32[]{:S(2)}) async-start(bf16[16,16,4224]{2,1,0:T(8,128)(2,1)} %select_rows.1), calls=%async_computation.3 | async-start | bytes 4325376 | tf_op jit(solution)/shard_map/all_to_all | solution.py:236
  87.8 1.9 %collective-permute-start.4 = (bf16[192,4096]{1,0:T(8,128)(2,1)}, bf16[192,4096]{1,0:T(8,128)(2,1)S(1)}, u32[]{:S(2)}, u32[]{:S(2)}) collective-permute-start(bf16[192,4096]{1,0:T(8,128)(2,1)} %ga_ref.1), channel_id=1, source_target_pairs={{0,16},{16,0},{1,17},{17,1},{2,18},{18,2},{3,19},{19,3},{4,20},{20... | collective-permute-start | bytes 4718600 | tf_op jit(solution)/shard_map/ppermute | solution.py:272
  89.7 2.4 %collective-permute-start.5 = (bf16[192,4096]{1,0:T(8,128)(2,1)}, bf16[192,4096]{1,0:T(8,128)(2,1)S(1)}, u32[]{:S(2)}, u32[]{:S(2)}) collective-permute-start(bf16[192,4096]{1,0:T(8,128)(2,1)} %ua_ref.1), channel_id=1, source_target_pairs={{0,16},{16,0},{1,17},{17,1},{2,18},{18,2},{3,19},{19,3},{4,20},{20... | collective-permute-start | bytes 4718600 | tf_op jit(solution)/shard_map/ppermute | solution.py:272
  92.1 1.9 %collective-permute-start.6 = (bf16[4,1536,128]{2,1,0:T(8,128)(2,1)}, bf16[4,1536,128]{2,1,0:T(8,128)(2,1)}, u32[]{:S(2)}, u32[]{:S(2)}) collective-permute-start(bf16[4,1536,128]{2,1,0:T(8,128)(2,1)} %refs_0_.1), channel_id=1, source_target_pairs={{0,16},{16,0},{1,17},{17,1},{2,18},{18,2},{3,19},{19,3},{4,20},{20... | collective-permute-start | bytes 4718600 | tf_op jit(solution)/shard_map/ppermute | solution.py:272
  94.1 2.4 %collective-permute-start.7 = (bf16[4,1536,128]{2,1,0:T(8,128)(2,1)}, bf16[4,1536,128]{2,1,0:T(8,128)(2,1)}, u32[]{:S(2)}, u32[]{:S(2)}) collective-permute-start(bf16[4,1536,128]{2,1,0:T(8,128)(2,1)} %collective-permute-done.1.refs_1_), channel_id=1, source_target_pairs={{0,16},{16,0},{1,17},{17,1},{2,18},{18,2},{3,19},{19,3},{4,20},{20... | collective-permute-start | bytes 4718600 | tf_op jit(solution)/shard_map/ppermute | solution.py:272
  96.5 1.9 %collective-permute-start.8 = (bf16[4,1536,128]{2,1,0:T(8,128)(2,1)}, bf16[4,1536,128]{2,1,0:T(8,128)(2,1)}, u32[]{:S(2)}, u32[]{:S(2)}) collective-permute-start(bf16[4,1536,128]{2,1,0:T(8,128)(2,1)} %copy-done.6), channel_id=1, source_target_pairs={{0,16},{16,0},{1,17},{17,1},{2,18},{18,2},{3,19},{19,3},{4,20},{20... | collective-permute-start | bytes 4718600 | tf_op jit(solution)/shard_map/ppermute | solution.py:272
  98.4 2.4 %collective-permute-start.9 = (bf16[2,1536,128]{2,1,0:T(8,128)(2,1)}, bf16[2,1536,128]{2,1,0:T(8,128)(2,1)S(1)}, u32[]{:S(2)}, u32[]{:S(2)}) collective-permute-start(bf16[2,1536,128]{2,1,0:T(8,128)(2,1)} %collective-permute-done.2.refs_3_), channel_id=1, source_target_pairs={{0,16},{16,0},{1,17},{17,1},{2,18},{18,2},{3,19},{19,3},{4,20},{20... | collective-permute-start | bytes 2359304 | tf_op jit(solution)/shard_map/ppermute | solution.py:272
  100.9 1.2 copy-done.5
  102.1 1.9 %collective-permute-start.10 = (bf16[2,1536,128]{2,1,0:T(8,128)(2,1)}, bf16[2,1536,128]{2,1,0:T(8,128)(2,1)}, u32[]{:S(2)}, u32[]{:S(2)}) collective-permute-start(bf16[2,1536,128]{2,1,0:T(8,128)(2,1)} %collective-permute-done.3.refs_4_), channel_id=1, source_target_pairs={{0,16},{16,0},{1,17},{17,1},{2,18},{18,2},{3,19},{19,3},{4,20},{20... | collective-permute-start | bytes 2359304 | tf_op jit(solution)/shard_map/ppermute | solution.py:272
  104.0 14.4 %all-to-all-done.3 = bf16[16,16,4224]{2,1,0:T(8,128)(2,1)S(1)} async-done(((bf16[16,16,4224]{2,1,0:T(8,128)(2,1)}), bf16[16,16,4224]{2,1,0:T(8,128)(2,1)S(1)}, u32[]{:S(2)}, u32[]{:S(2)}) %all-to-all-start.3) | async-done | bytes 2162720 | tf_op jit(solution)/shard_map/all_to_all | solution.py:236
  118.4 5.9 %gate_up.1 = (bf16[16,64,384]{2,1,0:T(8,128)(2,1)}, bf16[4,64,128]{2,1,0:T(8,128)(2,1)S(1)}) custom-call(s32[1]{0:T(128)} %bitcast.9.core_ref, bf16[256,4224]{1,0:T(8,128)(2,1)S(1)} %bitcast.28, bf16[192,4096]{1,0:T(8,128)(2,1)} %ga_ref.1, bf16[192,4096]{1,0:T(8,128)(2,1)} %ua_ref.1, bf16[192,4096]{1,0:T(8,128)(2,1)} %copy-done.4, bf16[192,4096]{1,0:T(8,128)(2,1)} %copy-done.5), custom_call_target="tpu_custom_call" | custom-call | tf_op jit(solution)/shard_map/gate_up/pallas_call | solution.py:342
  124.3 3.9 %all-to-all-start.4 = ((bf16[16,64,384]{2,1,0:T(8,128)(2,1)}), bf16[16,64,384]{2,1,0:T(8,128)(2,1)S(1)}, u32[]{:S(2)}, u32[]{:S(2)}) async-start(bf16[16,64,384]{2,1,0:T(8,128)(2,1)} %get-tuple-element.22), calls=%async_computation.4 | async-start | bytes 1572864 | tf_op jit(solution)/shard_map/all_to_all | solution.py:236
  128.2 0.1 pad_add_fusion.place_ref
  128.3 11.8 %all-to-all-done.4.act_ref = bf16[16,64,384]{2,1,0:T(8,128)(2,1)S(1)} async-done(((bf16[16,64,384]{2,1,0:T(8,128)(2,1)}), bf16[16,64,384]{2,1,0:T(8,128)(2,1)S(1)}, u32[]{:S(2)}, u32[]{:S(2)}) %all-to-all-start.4) | async-done | bytes 786464 | tf_op jit(solution)/shard_map/all_to_all | solution.py:236
  140.1 6.7 %down.1 = bf16[64,2,1024]{2,1,0:T(2,128)(2,1)} custom-call(s32[3]{0:T(128)S(1)} %pad_add_fusion.place_ref, bf16[16,64,384]{2,1,0:T(8,128)(2,1)S(1)} %all-to-all-done.4.act_ref, bf16[4,64,128]{2,1,0:T(8,128)(2,1)S(1)} %get-tuple-element.23.gate_ref, bf16[4,1536,128]{2,1,0:T(8,128)(2,1)} %refs_0_.1, bf16[4,1536,128]{2,1,0:T(8,128)(2,1)} %collective-permute-done.1.refs_1_, ...), custom_call_target="tpu_custom_call" | custom-call | tf_op jit(solution)/shard_map/down/pallas_call | solution.py:355
  146.8 13.3 %all-to-all-start.5 = ((bf16[64,2,1024]{2,1,0:T(2,128)(2,1)}), bf16[64,2,1024]{2,1,0:T(2,128)(2,1)S(1)}, u32[]{:S(2)}, u32[]{:S(2)}) async-start(bf16[64,2,1024]{2,1,0:T(2,128)(2,1)} %down.1), calls=%async_computation.5 | async-start | bytes 524288 | tf_op jit(solution)/shard_map/all_to_all | solution.py:236
  160.2 0.6 copy.35
  160.8 20.7 %all-to-all-done.5.landed_ref = bf16[64,2,1024]{2,1,0:T(2,128)(2,1)S(1)} async-done(((bf16[64,2,1024]{2,1,0:T(2,128)(2,1)}), bf16[64,2,1024]{2,1,0:T(2,128)(2,1)S(1)}, u32[]{:S(2)}, u32[]{:S(2)}) %all-to-all-start.5) | async-done | bytes 262176 | tf_op jit(solution)/shard_map/all_to_all | solution.py:236
  181.5 1.3 layer_out.1
  (29 shorter events, 0.1 us)
Async XLA Ops:
  0.6 34.3 %copy-start.2 = (s32[32,1]{0,1:T(1,128)S(1)}, s32[32,1]{0,1:T(1,128)}, u32[]{:S(2)}) copy-start(s32[32,1]{0,1:T(1,128)} %param.22) | copy-start | bytes 388
  0.6 34.3 %copy-start.1 = (f32[4096]{0:T(1024)S(1)}, f32[4096]{0:T(1024)}, u32[]{:S(2)}) copy-start(f32[4096]{0:T(1024)} %param.17) | copy-start | bytes 49156
  2.2 17.3 %all-to-all-start = ((bf16[32,48,128]{2,1,0:T(8,128)(2,1)}), bf16[32,48,128]{2,1,0:T(8,128)(2,1)S(1)}, u32[]{:S(2)}, u32[]{:S(2)}) async-start(bf16[32,48,128]{2,1,0:T(8,128)(2,1)} %get-tuple-element.16), calls=%async_computation | async-start | bytes 786432 | tf_op jit(solution)/shard_map/all_to_all | solution.py:236
  12.7 0.9 copy-start
  13.7 22.6 %copy-start.3 = (bf16[4,1536,128]{2,1,0:T(8,128)(2,1)S(1)}, bf16[4,1536,128]{2,1,0:T(8,128)(2,1)}, u32[]{:S(2)}) copy-start(bf16[4,1536,128]{2,1,0:T(8,128)(2,1)} %refs_0_.1) | copy-start | bytes 4718596
  22.1 12.8 %all-to-all-start.1 = ((bf16[32,32,128]{2,1,0:T(8,128)(2,1)}), bf16[32,32,128]{2,1,0:T(8,128)(2,1)S(1)}, u32[]{:S(2)}, u32[]{:S(2)}) async-start(bf16[32,32,128]{2,1,0:T(8,128)(2,1)} %guest_attention.1), calls=%async_computation.1 | async-start | bytes 524288 | tf_op jit(solution)/shard_map/all_to_all | solution.py:236
  36.3 45.6 %collective-permute-start = (bf16[4,1536,128]{2,1,0:T(8,128)(2,1)S(1)}, bf16[4,1536,128]{2,1,0:T(8,128)(2,1)S(1)}, u32[]{:S(2)}, u32[]{:S(2)}) collective-permute-start(bf16[4,1536,128]{2,1,0:T(8,128)(2,1)S(1)} %copy-done.3), channel_id=1, source_target_pairs={{0,480},{16,176},{32,384},{48,208},{64,416},{80,240},{96,448},{112... | collective-permute-start | bytes 4718600 | tf_op jit(solution)/shard_map/ppermute | solution.py:324
  39.9 42.0 %collective-permute-start.1 = (bf16[4,1536,128]{2,1,0:T(8,128)(2,1)S(1)}, bf16[4,1536,128]{2,1,0:T(8,128)(2,1)}, u32[]{:S(2)}, u32[]{:S(2)}) collective-permute-start(bf16[4,1536,128]{2,1,0:T(8,128)(2,1)S(1)} %copy-done.3), channel_id=1, source_target_pairs={{0,384},{16,144},{128,0},{144,272},{256,128},{272,400},{384,256},{... | collective-permute-start | bytes 4718600 | tf_op jit(solution)/shard_map/ppermute | solution.py:325
  42.7 36.3 %all-to-all-start.2 = ((bf16[16,80,128]{2,1,0:T(8,128)(2,1)}), bf16[16,80,128]{2,1,0:T(8,128)(2,1)S(1)}, u32[]{:S(2)}, u32[]{:S(2)}) async-start(bf16[16,80,128]{2,1,0:T(8,128)(2,1)} %get-tuple-element.18), calls=%async_computation.2 | async-start | bytes 655360 | tf_op jit(solution)/shard_map/all_to_all | solution.py:236
  59.2 21.6 %collective-permute-start.2 = (bf16[2,1536,128]{2,1,0:T(8,128)(2,1)}, bf16[2,1536,128]{2,1,0:T(8,128)(2,1)}, u32[]{:S(2)}, u32[]{:S(2)}) collective-permute-start(bf16[2,1536,128]{2,1,0:T(8,128)(2,1)} %get-tuple-element.29), channel_id=1, source_target_pairs={{0,96},{16,48},{32,0},{48,80},{64,32},{80,112},{96,64},{112,16},{1... | collective-permute-start | bytes 2359304 | tf_op jit(solution)/shard_map/ppermute | solution.py:326
  61.5 20.3 %collective-permute-start.3 = (bf16[2,1536,128]{2,1,0:T(8,128)(2,1)}, bf16[2,1536,128]{2,1,0:T(8,128)(2,1)}, u32[]{:S(2)}, u32[]{:S(2)}) collective-permute-start(bf16[2,1536,128]{2,1,0:T(8,128)(2,1)} %get-tuple-element.28), channel_id=1, source_target_pairs={{0,96},{16,48},{32,0},{48,80},{64,32},{80,112},{96,64},{112,16},{1... | collective-permute-start | bytes 2359304 | tf_op jit(solution)/shard_map/ppermute | solution.py:326
  81.9 1.2 copy-start.6
  83.0 35.3 %all-to-all-start.3 = ((bf16[16,16,4224]{2,1,0:T(8,128)(2,1)}), bf16[16,16,4224]{2,1,0:T(8,128)(2,1)S(1)}, u32[]{:S(2)}, u32[]{:S(2)}) async-start(bf16[16,16,4224]{2,1,0:T(8,128)(2,1)} %select_rows.1), calls=%async_computation.3 | async-start | bytes 4325376 | tf_op jit(solution)/shard_map/all_to_all | solution.py:236
  87.8 10.6 %collective-permute-start.4 = (bf16[192,4096]{1,0:T(8,128)(2,1)}, bf16[192,4096]{1,0:T(8,128)(2,1)S(1)}, u32[]{:S(2)}, u32[]{:S(2)}) collective-permute-start(bf16[192,4096]{1,0:T(8,128)(2,1)} %ga_ref.1), channel_id=1, source_target_pairs={{0,16},{16,0},{1,17},{17,1},{2,18},{18,2},{3,19},{19,3},{4,20},{20... | collective-permute-start | bytes 4718600 | tf_op jit(solution)/shard_map/ppermute | solution.py:272
  89.7 11.1 %collective-permute-start.5 = (bf16[192,4096]{1,0:T(8,128)(2,1)}, bf16[192,4096]{1,0:T(8,128)(2,1)S(1)}, u32[]{:S(2)}, u32[]{:S(2)}) collective-permute-start(bf16[192,4096]{1,0:T(8,128)(2,1)} %ua_ref.1), channel_id=1, source_target_pairs={{0,16},{16,0},{1,17},{17,1},{2,18},{18,2},{3,19},{19,3},{4,20},{20... | collective-permute-start | bytes 4718600 | tf_op jit(solution)/shard_map/ppermute | solution.py:272
  92.1 36.1 %collective-permute-start.6 = (bf16[4,1536,128]{2,1,0:T(8,128)(2,1)}, bf16[4,1536,128]{2,1,0:T(8,128)(2,1)}, u32[]{:S(2)}, u32[]{:S(2)}) collective-permute-start(bf16[4,1536,128]{2,1,0:T(8,128)(2,1)} %refs_0_.1), channel_id=1, source_target_pairs={{0,16},{16,0},{1,17},{17,1},{2,18},{18,2},{3,19},{19,3},{4,20},{20... | collective-permute-start | bytes 4718600 | tf_op jit(solution)/shard_map/ppermute | solution.py:272
  94.1 34.2 %collective-permute-start.7 = (bf16[4,1536,128]{2,1,0:T(8,128)(2,1)}, bf16[4,1536,128]{2,1,0:T(8,128)(2,1)}, u32[]{:S(2)}, u32[]{:S(2)}) collective-permute-start(bf16[4,1536,128]{2,1,0:T(8,128)(2,1)} %collective-permute-done.1.refs_1_), channel_id=1, source_target_pairs={{0,16},{16,0},{1,17},{17,1},{2,18},{18,2},{3,19},{19,3},{4,20},{20... | collective-permute-start | bytes 4718600 | tf_op jit(solution)/shard_map/ppermute | solution.py:272
  96.5 31.8 %collective-permute-start.8 = (bf16[4,1536,128]{2,1,0:T(8,128)(2,1)}, bf16[4,1536,128]{2,1,0:T(8,128)(2,1)}, u32[]{:S(2)}, u32[]{:S(2)}) collective-permute-start(bf16[4,1536,128]{2,1,0:T(8,128)(2,1)} %copy-done.6), channel_id=1, source_target_pairs={{0,16},{16,0},{1,17},{17,1},{2,18},{18,2},{3,19},{19,3},{4,20},{20... | collective-permute-start | bytes 4718600 | tf_op jit(solution)/shard_map/ppermute | solution.py:272
  98.4 2.4 %copy-start.4 = (bf16[192,4096]{1,0:T(8,128)(2,1)}, bf16[192,4096]{1,0:T(8,128)(2,1)S(1)}, u32[]{:S(2)}) copy-start(bf16[192,4096]{1,0:T(8,128)(2,1)S(1)} %collective-permute-done.4.gb_ref) | copy-start | bytes 4718596
  98.4 29.8 %collective-permute-start.9 = (bf16[2,1536,128]{2,1,0:T(8,128)(2,1)}, bf16[2,1536,128]{2,1,0:T(8,128)(2,1)S(1)}, u32[]{:S(2)}, u32[]{:S(2)}) collective-permute-start(bf16[2,1536,128]{2,1,0:T(8,128)(2,1)} %collective-permute-done.2.refs_3_), channel_id=1, source_target_pairs={{0,16},{16,0},{1,17},{17,1},{2,18},{18,2},{3,19},{19,3},{4,20},{20... | collective-permute-start | bytes 2359304 | tf_op jit(solution)/shard_map/ppermute | solution.py:272
  100.9 1.2 copy-start.5
  102.1 26.2 %collective-permute-start.10 = (bf16[2,1536,128]{2,1,0:T(8,128)(2,1)}, bf16[2,1536,128]{2,1,0:T(8,128)(2,1)}, u32[]{:S(2)}, u32[]{:S(2)}) collective-permute-start(bf16[2,1536,128]{2,1,0:T(8,128)(2,1)} %collective-permute-done.3.refs_4_), channel_id=1, source_target_pairs={{0,16},{16,0},{1,17},{17,1},{2,18},{18,2},{3,19},{19,3},{4,20},{20... | collective-permute-start | bytes 2359304 | tf_op jit(solution)/shard_map/ppermute | solution.py:272
  124.3 15.8 %all-to-all-start.4 = ((bf16[16,64,384]{2,1,0:T(8,128)(2,1)}), bf16[16,64,384]{2,1,0:T(8,128)(2,1)S(1)}, u32[]{:S(2)}, u32[]{:S(2)}) async-start(bf16[16,64,384]{2,1,0:T(8,128)(2,1)} %get-tuple-element.22), calls=%async_computation.4 | async-start | bytes 1572864 | tf_op jit(solution)/shard_map/all_to_all | solution.py:236
  128.3 11.8 %copy-start.7 = (bf16[2,1536,128]{2,1,0:T(8,128)(2,1)}, bf16[2,1536,128]{2,1,0:T(8,128)(2,1)S(1)}, u32[]{:S(2)}) copy-start(bf16[2,1536,128]{2,1,0:T(8,128)(2,1)S(1)} %collective-permute-done.9.refs_8_) | copy-start | bytes 2359300
  146.8 34.7 %all-to-all-start.5 = ((bf16[64,2,1024]{2,1,0:T(2,128)(2,1)}), bf16[64,2,1024]{2,1,0:T(2,128)(2,1)S(1)}, u32[]{:S(2)}, u32[]{:S(2)}) async-start(bf16[64,2,1024]{2,1,0:T(2,128)(2,1)} %down.1), calls=%async_computation.5 | async-start | bytes 524288 | tf_op jit(solution)/shard_map/all_to_all | solution.py:236

commit v3 on v2

--- a/solution.py
+++ b/solution.py
@@ -96,20 +96,24 @@
 
 
 def token_kernel(
-    me_ref, from_ref, own_ref, back_ref, resid_ref, gain_ref, meta_ref, attn_ref, stream_ref, out_ref
+    me_ref, from_ref, own_ref, back_ref, resid_ref, gain_ref, meta_ref, attn_ref, stream_ref, out_ref, line_ref
 ):
     root = from_ref[me_ref[0]]
     rows = (own_ref[...], back_ref[root])
     for r in range(2):
-        attn_ref[r] = rows[r]
-        stream = resid_ref[r].astype(jnp.float32) + rows[r].astype(jnp.float32)
-        stream_ref[r] = stream
+        attn = rows[r].astype(jnp.float32)
+        stream = resid_ref[r].astype(jnp.float32) + attn
+        for h in range(HEADS):
+            at = slice(h * HEAD, (h + 1) * HEAD)
+            line_ref[r : r + 1, at] = attn[h : h + 1]
+            stream_ref[r : r + 1, at] = stream[h : h + 1]
         square = jnp.sum(jnp.sum(stream * stream, axis=1, keepdims=True), axis=0, keepdims=True)
         normed = (stream * lax.rsqrt(square / D + 1e-06) * gain_ref[...]).astype(jnp.bfloat16)
         for e in range(out_ref.shape[0]):
             out_ref[e, r * 32 : (r + 1) * 32] = normed
     for e in range(out_ref.shape[0]):
         out_ref[e, 64:80] = meta_ref[...]
+    attn_ref[...] = line_ref[...].astype(jnp.bfloat16)
 
 
 def select_kernel(expert_ref, rows_ref, meta_ref, out_ref):
@@ -168,8 +172,8 @@
     for x in range(LOCAL):
         sources = []
         for c in range(2):
-            own, by_x, by_both, *by_y = w_refs[5 * c : 5 * c + 5]
-            sources += [own.at[x], by_x.at[x], by_y[x // 2].at[x % 2], by_both.at[x]]
+            own, by_x, by_y, *by_both = w_refs[5 * c : 5 * c + 5]
+            sources += [own.at[x], by_x.at[x], by_y.at[x], by_both[x // 2].at[x % 2]]
         copies.append(
             [
                 pltpu.make_async_copy(source, held_ref.at[x, i], sems.at[x, i])
@@ -311,19 +315,20 @@
     attn, stream, tokens = pl.pallas_call(
         token_kernel,
         out_shape=(
-            jax.ShapeDtypeStruct((2, HEADS, HEAD), bf16),
-            jax.ShapeDtypeStruct((2, HEADS, HEAD), f32),
+            jax.ShapeDtypeStruct((2, D), bf16),
+            jax.ShapeDtypeStruct((2, D), f32),
             jax.ShapeDtypeStruct((owners, 80, HEAD), bf16),
         ),
         in_specs=[SMEM, SMEM] + [VMEM] * 5,
         out_specs=(VMEM, VMEM, VMEM),
+        scratch_shapes=[pltpu.VMEM((2, D), f32)],
         compiler_params=params(8),
         name="tokens",
     )(me, source, own, back, resid.reshape(2, HEADS, HEAD), norm_gain.reshape(HEADS, HEAD), meta)
     later = tie(stream, w_down)
-    by_both = lax.ppermute(later, PLANE, far)
     by_x = lax.ppermute(later, X + ("c",), onward)
-    by_y = [lax.ppermute(a, Y + ("c",), onward) for a in (later[:2], later[2:])]
+    by_y = lax.ppermute(later, Y + ("c",), onward)
+    by_both = [lax.ppermute(a, PLANE, far) for a in (later[:2], later[2:])]
 
     arrived = exchange(tokens, ("zl", "zh"))
     chosen = pl.pallas_call(
@@ -336,7 +341,7 @@
     )(expert, arrived[:, :64].reshape(owners, 2 * D), arrived[:, 64:])
     chosen, by_both, by_x, by_y = lax.optimization_barrier((chosen, by_both, by_x, by_y))
     gate_b, up_b = swap(w_gate), swap(w_up)
-    downs = [w_down, by_x, by_both] + by_y
+    downs = [w_down, by_x, by_y] + by_both
     downs += [swap(a) for a in downs]
     chosen = exchange(chosen, XY).reshape(16 * owners, D + HEAD)
     hidden, gates = pl.pallas_call(
@@ -372,8 +377,8 @@
         out_specs=VMEM,
         compiler_params=params(4),
         name="layer_out",
-    )(place, landed, stream.reshape(2, D))
-    return attn.reshape(2, D), layer_out
+    )(place, landed, stream)
+    return attn, layer_out
 
 
 def solution(mesh):

time: 184 us -> 182 us (0.989)
  blocking collectives: 0 us -> 35.1 us
  waiting for transfers between devices: 76.2 us -> 54.1 us
  starting transfers between devices: 75.3 us -> 62.2 us
    all_to_all x0 -> x1, blocking collectives: none -> 35.1 us  [exchange(): return lax.all_to_all(a, axes, split_axis=0, concat_axis=0, tiled=True)]
    all_to_all x6 -> x5, waiting for transfers between devices: 75.2 us -> 52.6 us  [exchange(): return lax.all_to_all(a, axes, split_axis=0, concat_axis=0, tiled=True)]
    all_to_all x6 -> x5, starting transfers between devices: 48.4 us -> 34.8 us  [exchange(): return lax.all_to_all(a, axes, split_axis=0, concat_axis=0, tiled=True)]
    unnamed x20 -> x18, local copies, waits for them, and re-layouts: 4.86 us -> 4.22 us
  transfers between devices with their start and end apart: 17 -> 16, of which waited for: 7 -> 6; matrix products, arithmetic and copies ran while one was open for 3% -> 2% of each run, Pallas kernels for 4% -> 4%
where the time goes in v3:
time: 182 us; the launch traced here: 181 us
  starting transfers between devices  62.2 us (34%)
  waiting for transfers between devices  54.1 us (30%)
  blocking collectives  35.1 us (19%)
  Pallas kernels  20.9 us (11%)
  local copies, waits for them, and re-layouts  5.77 us (3%)
    all_to_all x5, waiting for transfers between devices, exchange(): return lax.all_to_all(a, axes, split_axis=0, concat_axis=0, tiled=True)  52.6 us
    all_to_all x1, blocking collectives, exchange(): return lax.all_to_all(a, axes, split_axis=0, concat_axis=0, tiled=True)  35.1 us
    all_to_all x5, starting transfers between devices, exchange(): return lax.all_to_all(a, axes, split_axis=0, concat_axis=0, tiled=True)  34.8 us
    ppermute x7, starting transfers between devices, on_device(): swap = lambda a: lax.ppermute(a, 'c', [(0, 1), (1, 0)])  14.9 us
    ppermute x2, starting transfers between devices, on_device(): by_both = [lax.ppermute(a, PLANE, far) for a in (later[:2], later[2:])]  6.46 us
    pallas_call x1, Pallas kernels, on_device(): pl.pallas_call(down_kernel, out_shape=jax.ShapeDtypeStruct((64, 2, 8 * HE...  6.02 us
    pallas_call x1, Pallas kernels, on_device(): pl.pallas_call(up_kernel, out_shape=(jax.ShapeDtypeStruct((16, 64, 2 * UN...  5.87 us
    unnamed x18, local copies, waits for them, and re-layouts  4.22 us
  transfers between devices with their start and end apart: 16, of which 6 were waited for; matrix products, arithmetic and copies ran while one was open for 2% of the time, Pallas kernels for 4%

profile of v3, /device:TPU:32, one launch (start us, length us, event | category | flops | bytes accessed | tf_op | source)
XLA Modules:
  0.0 181.4 jit_solution(7282010746209635796)
XLA Ops:
  0.6 0.0 copy-start.2
  0.7 1.5 ask.1
  2.2 7.3 %all-to-all-start = ((bf16[32,48,128]{2,1,0:T(8,128)(2,1)}), bf16[32,48,128]{2,1,0:T(8,128)(2,1)S(1)}, u32[]{:S(2)}, u32[]{:S(2)}) async-start(bf16[32,48,128]{2,1,0:T(8,128)(2,1)} %get-tuple-element.16), calls=%async_computation | async-start | bytes 786432 | tf_op jit(solution)/shard_map/all_to_all | solution.py:240
  9.5 0.8 select_reduce_fusion
  10.3 0.1 copy.22
  11.0 0.7 copy.30
  11.8 0.8 broadcast_compare_fusion
  12.6 0.1 copy.24
  12.7 0.1 copy.23
  12.7 0.9 copy-done
  13.6 0.6 resident_attention.1.own_ref
  14.2 5.2 %all-to-all-done.asked_ref = bf16[32,48,128]{2,1,0:T(8,128)(2,1)S(1)} async-done(((bf16[32,48,128]{2,1,0:T(8,128)(2,1)}), bf16[32,48,128]{2,1,0:T(8,128)(2,1)S(1)}, u32[]{:S(2)}, u32[]{:S(2)}) %all-to-all-start) | async-done | bytes 393248 | tf_op jit(solution)/shard_map/all_to_all | solution.py:240
  19.5 2.6 %guest_attention.1 = bf16[32,32,128]{2,1,0:T(8,128)(2,1)} custom-call(s32[1]{0:T(128)} %bitcast.me_ref, s32[32]{0:T(128)} %bitcast.25, s32[32]{0:T(128)} %bitcast.32, bf16[32,48,128]{2,1,0:T(8,128)(2,1)S(1)} %all-to-all-done.asked_ref, bf16[256,512]{1,0:T(8,128)(2,1)} %bitcast.28), custom_call_target="tpu_custom_call" | custom-call | tf_op jit(solution)/shard_map/guest_attention/pallas_call | solution.py:305
  22.1 3.9 %all-to-all-start.1 = ((bf16[32,32,128]{2,1,0:T(8,128)(2,1)}), bf16[32,32,128]{2,1,0:T(8,128)(2,1)S(1)}, u32[]{:S(2)}, u32[]{:S(2)}) async-start(bf16[32,32,128]{2,1,0:T(8,128)(2,1)} %guest_attention.1), calls=%async_computation.1 | async-start | bytes 524288 | tf_op jit(solution)/shard_map/all_to_all | solution.py:240
  26.0 0.1 fusion.4.meta_ref
  26.1 8.8 %all-to-all-done.1.back_ref = bf16[32,32,128]{2,1,0:T(8,128)(2,1)S(1)} async-done(((bf16[32,32,128]{2,1,0:T(8,128)(2,1)}), bf16[32,32,128]{2,1,0:T(8,128)(2,1)S(1)}, u32[]{:S(2)}, u32[]{:S(2)}) %all-to-all-start.1) | async-done | bytes 262176 | tf_op jit(solution)/shard_map/all_to_all | solution.py:240
  34.9 1.4 tokens.1
  36.3 3.0 %collective-permute-start.2 = (bf16[4,1536,128]{2,1,0:T(8,128)(2,1)S(1)}, bf16[4,1536,128]{2,1,0:T(8,128)(2,1)S(1)}, u32[]{:S(2)}, u32[]{:S(2)}) collective-permute-start(bf16[4,1536,128]{2,1,0:T(8,128)(2,1)S(1)} %copy-done.3), channel_id=1, source_target_pairs={{0,384},{16,144},{128,0},{144,272},{256,128},{272,400},{384,256},{... | collective-permute-start | bytes 4718600 | tf_op jit(solution)/shard_map/ppermute | solution.py:329
  39.3 3.1 %collective-permute-start.3 = (bf16[4,1536,128]{2,1,0:T(8,128)(2,1)S(1)}, bf16[4,1536,128]{2,1,0:T(8,128)(2,1)}, u32[]{:S(2)}, u32[]{:S(2)}) collective-permute-start(bf16[4,1536,128]{2,1,0:T(8,128)(2,1)S(1)} %copy-done.3), channel_id=1, source_target_pairs={{0,96},{16,48},{32,0},{48,80},{64,32},{80,112},{96,64},{112,16},{1... | collective-permute-start | bytes 4718600 | tf_op jit(solution)/shard_map/ppermute | solution.py:330
  42.4 15.2 %all-to-all-start.2 = ((bf16[16,80,128]{2,1,0:T(8,128)(2,1)}), bf16[16,80,128]{2,1,0:T(8,128)(2,1)S(1)}, u32[]{:S(2)}, u32[]{:S(2)}) async-start(bf16[16,80,128]{2,1,0:T(8,128)(2,1)} %get-tuple-element.18), calls=%async_computation.2 | async-start | bytes 655360 | tf_op jit(solution)/shard_map/all_to_all | solution.py:240
  57.6 1.3 fusion.5
  58.9 2.6 %collective-permute-start = (bf16[2,1536,128]{2,1,0:T(8,128)(2,1)}, bf16[2,1536,128]{2,1,0:T(8,128)(2,1)}, u32[]{:S(2)}, u32[]{:S(2)}) collective-permute-start(bf16[2,1536,128]{2,1,0:T(8,128)(2,1)} %get-tuple-element.29), channel_id=1, source_target_pairs={{0,480},{16,176},{32,384},{48,208},{64,416},{80,240},{96,448},{112... | collective-permute-start | bytes 2359304 | tf_op jit(solution)/shard_map/ppermute | solution.py:331
  61.5 3.8 %collective-permute-start.1 = (bf16[2,1536,128]{2,1,0:T(8,128)(2,1)}, bf16[2,1536,128]{2,1,0:T(8,128)(2,1)}, u32[]{:S(2)}, u32[]{:S(2)}) collective-permute-start(bf16[2,1536,128]{2,1,0:T(8,128)(2,1)} %get-tuple-element.28), channel_id=1, source_target_pairs={{0,480},{16,176},{32,384},{48,208},{64,416},{80,240},{96,448},{112... | collective-permute-start | bytes 2359304 | tf_op jit(solution)/shard_map/ppermute | solution.py:331
  65.4 13.7 %all-to-all-done.2 = bf16[16,80,128]{2,1,0:T(8,128)(2,1)S(1)} async-done(((bf16[16,80,128]{2,1,0:T(8,128)(2,1)}), bf16[16,80,128]{2,1,0:T(8,128)(2,1)S(1)}, u32[]{:S(2)}, u32[]{:S(2)}) %all-to-all-start.2) | async-done | bytes 327712 | tf_op jit(solution)/shard_map/all_to_all | solution.py:240
  79.1 0.2 copy.29
  79.3 1.6 select_rows.1
  80.9 1.5 collective-permute-done.1.refs_4_
  82.4 1.2 copy-done.6
  83.6 4.5 %all-to-all-start.3 = ((bf16[16,16,4224]{2,1,0:T(8,128)(2,1)}), bf16[16,16,4224]{2,1,0:T(8,128)(2,1)S(1)}, u32[]{:S(2)}, u32[]{:S(2)}) async-start(bf16[16,16,4224]{2,1,0:T(8,128)(2,1)} %select_rows.1), calls=%async_computation.3 | async-start | bytes 4325376 | tf_op jit(solution)/shard_map/all_to_all | solution.py:240
  88.1 1.9 %collective-permute-start.4 = (bf16[192,4096]{1,0:T(8,128)(2,1)}, bf16[192,4096]{1,0:T(8,128)(2,1)S(1)}, u32[]{:S(2)}, u32[]{:S(2)}) collective-permute-start(bf16[192,4096]{1,0:T(8,128)(2,1)} %ga_ref.1), channel_id=1, source_target_pairs={{0,16},{16,0},{1,17},{17,1},{2,18},{18,2},{3,19},{19,3},{4,20},{20... | collective-permute-start | bytes 4718600 | tf_op jit(solution)/shard_map/ppermute | solution.py:276
  90.1 2.4 %collective-permute-start.5 = (bf16[192,4096]{1,0:T(8,128)(2,1)}, bf16[192,4096]{1,0:T(8,128)(2,1)S(1)}, u32[]{:S(2)}, u32[]{:S(2)}) collective-permute-start(bf16[192,4096]{1,0:T(8,128)(2,1)} %ua_ref.1), channel_id=1, source_target_pairs={{0,16},{16,0},{1,17},{17,1},{2,18},{18,2},{3,19},{19,3},{4,20},{20... | collective-permute-start | bytes 4718600 | tf_op jit(solution)/shard_map/ppermute | solution.py:276
  92.5 1.9 %collective-permute-start.6 = (bf16[4,1536,128]{2,1,0:T(8,128)(2,1)}, bf16[4,1536,128]{2,1,0:T(8,128)(2,1)}, u32[]{:S(2)}, u32[]{:S(2)}) collective-permute-start(bf16[4,1536,128]{2,1,0:T(8,128)(2,1)} %refs_0_.1), channel_id=1, source_target_pairs={{0,16},{16,0},{1,17},{17,1},{2,18},{18,2},{3,19},{19,3},{4,20},{20... | collective-permute-start | bytes 4718600 | tf_op jit(solution)/shard_map/ppermute | solution.py:276
  94.4 2.4 %collective-permute-start.7 = (bf16[4,1536,128]{2,1,0:T(8,128)(2,1)}, bf16[4,1536,128]{2,1,0:T(8,128)(2,1)}, u32[]{:S(2)}, u32[]{:S(2)}) collective-permute-start(bf16[4,1536,128]{2,1,0:T(8,128)(2,1)} %copy-done.6), channel_id=1, source_target_pairs={{0,16},{16,0},{1,17},{17,1},{2,18},{18,2},{3,19},{19,3},{4,20},{20... | collective-permute-start | bytes 4718600 | tf_op jit(solution)/shard_map/ppermute | solution.py:276
  96.8 1.9 %collective-permute-start.8 = (bf16[4,1536,128]{2,1,0:T(8,128)(2,1)}, bf16[4,1536,128]{2,1,0:T(8,128)(2,1)}, u32[]{:S(2)}, u32[]{:S(2)}) collective-permute-start(bf16[4,1536,128]{2,1,0:T(8,128)(2,1)} %collective-permute-done.3.refs_2_), channel_id=1, source_target_pairs={{0,16},{16,0},{1,17},{17,1},{2,18},{18,2},{3,19},{19,3},{4,20},{20... | collective-permute-start | bytes 4718600 | tf_op jit(solution)/shard_map/ppermute | solution.py:276
  98.8 2.4 %collective-permute-start.9 = (bf16[2,1536,128]{2,1,0:T(8,128)(2,1)}, bf16[2,1536,128]{2,1,0:T(8,128)(2,1)S(1)}, u32[]{:S(2)}, u32[]{:S(2)}) collective-permute-start(bf16[2,1536,128]{2,1,0:T(8,128)(2,1)} %collective-permute-done.refs_3_), channel_id=1, source_target_pairs={{0,16},{16,0},{1,17},{17,1},{2,18},{18,2},{3,19},{19,3},{4,20},{20... | collective-permute-start | bytes 2359304 | tf_op jit(solution)/shard_map/ppermute | solution.py:276
  101.2 0.0 collective-permute-done.5.ub_ref
  101.2 1.2 copy-done.5
  102.4 1.9 %collective-permute-start.10 = (bf16[2,1536,128]{2,1,0:T(8,128)(2,1)}, bf16[2,1536,128]{2,1,0:T(8,128)(2,1)}, u32[]{:S(2)}, u32[]{:S(2)}) collective-permute-start(bf16[2,1536,128]{2,1,0:T(8,128)(2,1)} %collective-permute-done.1.refs_4_), channel_id=1, source_target_pairs={{0,16},{16,0},{1,17},{17,1},{2,18},{18,2},{3,19},{19,3},{4,20},{20... | collective-permute-start | bytes 2359304 | tf_op jit(solution)/shard_map/ppermute | solution.py:276
  104.3 13.3 %all-to-all-done.3 = bf16[16,16,4224]{2,1,0:T(8,128)(2,1)S(1)} async-done(((bf16[16,16,4224]{2,1,0:T(8,128)(2,1)}), bf16[16,16,4224]{2,1,0:T(8,128)(2,1)S(1)}, u32[]{:S(2)}, u32[]{:S(2)}) %all-to-all-start.3) | async-done | bytes 2162720 | tf_op jit(solution)/shard_map/all_to_all | solution.py:240
  117.6 5.9 %gate_up.1 = (bf16[16,64,384]{2,1,0:T(8,128)(2,1)}, bf16[4,64,128]{2,1,0:T(8,128)(2,1)S(1)}) custom-call(s32[1]{0:T(128)} %bitcast.9.core_ref, bf16[256,4224]{1,0:T(8,128)(2,1)S(1)} %bitcast.20, bf16[192,4096]{1,0:T(8,128)(2,1)} %ga_ref.1, bf16[192,4096]{1,0:T(8,128)(2,1)} %ua_ref.1, bf16[192,4096]{1,0:T(8,128)(2,1)} %copy-done.4, bf16[192,4096]{1,0:T(8,128)(2,1)} %copy-done.5), custom_call_target="tpu_custom_call" | custom-call | tf_op jit(solution)/shard_map/gate_up/pallas_call | solution.py:347
  123.5 3.8 %all-to-all-start.4 = ((bf16[16,64,384]{2,1,0:T(8,128)(2,1)}), bf16[16,64,384]{2,1,0:T(8,128)(2,1)S(1)}, u32[]{:S(2)}, u32[]{:S(2)}) async-start(bf16[16,64,384]{2,1,0:T(8,128)(2,1)} %get-tuple-element.22), calls=%async_computation.4 | async-start | bytes 1572864 | tf_op jit(solution)/shard_map/all_to_all | solution.py:240
  127.3 0.1 pad_add_fusion.place_ref
  127.4 0.0 collective-permute-done.9.refs_8_
  127.4 0.0 collective-permute-done.10.refs_9_
  127.5 11.6 %all-to-all-done.4.act_ref = bf16[16,64,384]{2,1,0:T(8,128)(2,1)S(1)} async-done(((bf16[16,64,384]{2,1,0:T(8,128)(2,1)}), bf16[16,64,384]{2,1,0:T(8,128)(2,1)S(1)}, u32[]{:S(2)}, u32[]{:S(2)}) %all-to-all-start.4) | async-done | bytes 786464 | tf_op jit(solution)/shard_map/all_to_all | solution.py:240
  139.0 6.0 %down.1 = bf16[64,2,1024]{2,1,0:T(2,128)(2,1)S(1)} custom-call(s32[3]{0:T(128)S(1)} %pad_add_fusion.place_ref, bf16[16,64,384]{2,1,0:T(8,128)(2,1)S(1)} %all-to-all-done.4.act_ref, bf16[4,64,128]{2,1,0:T(8,128)(2,1)S(1)} %get-tuple-element.23.gate_ref, bf16[4,1536,128]{2,1,0:T(8,128)(2,1)} %refs_0_.1, bf16[4,1536,128]{2,1,0:T(8,128)(2,1)} %copy-done.6, ...), custom_call_target="tpu_custom_call" | custom-call | tf_op jit(solution)/shard_map/down/pallas_call | solution.py:360
  145.1 35.1 %all_to_all.30.landed_ref = bf16[64,2,1024]{2,1,0:T(2,128)(2,1)S(1)} all-to-all(bf16[64,2,1024]{2,1,0:T(2,128)(2,1)S(1)} %down.1), channel_id=1, replica_groups=mesh['xh'=2,'xl'=2,'yh'=2,'yl'=2,'c'=2,'zh'=4,'zl'=4] {'xh','yh','zl','zh'}, dimensions={0} | all-to-all | bytes 524288 | tf_op jit(solution)/shard_map/all_to_all | solution.py:240
  180.2 1.3 layer_out.1
  (26 shorter events, 0.1 us)
Async XLA Ops:
  0.6 34.3 %copy-start.2 = (s32[32,1]{0,1:T(1,128)S(1)}, s32[32,1]{0,1:T(1,128)}, u32[]{:S(2)}) copy-start(s32[32,1]{0,1:T(1,128)} %param.22) | copy-start | bytes 388
  0.6 34.3 %copy-start.1 = (f32[4096]{0:T(1024)S(1)}, f32[4096]{0:T(1024)}, u32[]{:S(2)}) copy-start(f32[4096]{0:T(1024)} %param.17) | copy-start | bytes 49156
  2.2 17.3 %all-to-all-start = ((bf16[32,48,128]{2,1,0:T(8,128)(2,1)}), bf16[32,48,128]{2,1,0:T(8,128)(2,1)S(1)}, u32[]{:S(2)}, u32[]{:S(2)}) async-start(bf16[32,48,128]{2,1,0:T(8,128)(2,1)} %get-tuple-element.16), calls=%async_computation | async-start | bytes 786432 | tf_op jit(solution)/shard_map/all_to_all | solution.py:240
  12.7 0.9 copy-start
  13.6 22.7 %copy-start.3 = (bf16[4,1536,128]{2,1,0:T(8,128)(2,1)S(1)}, bf16[4,1536,128]{2,1,0:T(8,128)(2,1)}, u32[]{:S(2)}) copy-start(bf16[4,1536,128]{2,1,0:T(8,128)(2,1)} %refs_0_.1) | copy-start | bytes 4718596
  22.1 12.8 %all-to-all-start.1 = ((bf16[32,32,128]{2,1,0:T(8,128)(2,1)}), bf16[32,32,128]{2,1,0:T(8,128)(2,1)S(1)}, u32[]{:S(2)}, u32[]{:S(2)}) async-start(bf16[32,32,128]{2,1,0:T(8,128)(2,1)} %guest_attention.1), calls=%async_computation.1 | async-start | bytes 524288 | tf_op jit(solution)/shard_map/all_to_all | solution.py:240
  36.3 46.1 %collective-permute-start.2 = (bf16[4,1536,128]{2,1,0:T(8,128)(2,1)S(1)}, bf16[4,1536,128]{2,1,0:T(8,128)(2,1)S(1)}, u32[]{:S(2)}, u32[]{:S(2)}) collective-permute-start(bf16[4,1536,128]{2,1,0:T(8,128)(2,1)S(1)} %copy-done.3), channel_id=1, source_target_pairs={{0,384},{16,144},{128,0},{144,272},{256,128},{272,400},{384,256},{... | collective-permute-start | bytes 4718600 | tf_op jit(solution)/shard_map/ppermute | solution.py:329
  39.3 43.1 %collective-permute-start.3 = (bf16[4,1536,128]{2,1,0:T(8,128)(2,1)S(1)}, bf16[4,1536,128]{2,1,0:T(8,128)(2,1)}, u32[]{:S(2)}, u32[]{:S(2)}) collective-permute-start(bf16[4,1536,128]{2,1,0:T(8,128)(2,1)S(1)} %copy-done.3), channel_id=1, source_target_pairs={{0,96},{16,48},{32,0},{48,80},{64,32},{80,112},{96,64},{112,16},{1... | collective-permute-start | bytes 4718600 | tf_op jit(solution)/shard_map/ppermute | solution.py:330
  42.4 36.7 %all-to-all-start.2 = ((bf16[16,80,128]{2,1,0:T(8,128)(2,1)}), bf16[16,80,128]{2,1,0:T(8,128)(2,1)S(1)}, u32[]{:S(2)}, u32[]{:S(2)}) async-start(bf16[16,80,128]{2,1,0:T(8,128)(2,1)} %get-tuple-element.18), calls=%async_computation.2 | async-start | bytes 655360 | tf_op jit(solution)/shard_map/all_to_all | solution.py:240
  58.9 22.0 %collective-permute-start = (bf16[2,1536,128]{2,1,0:T(8,128)(2,1)}, bf16[2,1536,128]{2,1,0:T(8,128)(2,1)}, u32[]{:S(2)}, u32[]{:S(2)}) collective-permute-start(bf16[2,1536,128]{2,1,0:T(8,128)(2,1)} %get-tuple-element.29), channel_id=1, source_target_pairs={{0,480},{16,176},{32,384},{48,208},{64,416},{80,240},{96,448},{112... | collective-permute-start | bytes 2359304 | tf_op jit(solution)/shard_map/ppermute | solution.py:331
  61.5 20.9 %collective-permute-start.1 = (bf16[2,1536,128]{2,1,0:T(8,128)(2,1)}, bf16[2,1536,128]{2,1,0:T(8,128)(2,1)}, u32[]{:S(2)}, u32[]{:S(2)}) collective-permute-start(bf16[2,1536,128]{2,1,0:T(8,128)(2,1)} %get-tuple-element.28), channel_id=1, source_target_pairs={{0,480},{16,176},{32,384},{48,208},{64,416},{80,240},{96,448},{112... | collective-permute-start | bytes 2359304 | tf_op jit(solution)/shard_map/ppermute | solution.py:331
  82.4 1.2 copy-start.6
  83.6 34.1 %all-to-all-start.3 = ((bf16[16,16,4224]{2,1,0:T(8,128)(2,1)}), bf16[16,16,4224]{2,1,0:T(8,128)(2,1)S(1)}, u32[]{:S(2)}, u32[]{:S(2)}) async-start(bf16[16,16,4224]{2,1,0:T(8,128)(2,1)} %select_rows.1), calls=%async_computation.3 | async-start | bytes 4325376 | tf_op jit(solution)/shard_map/all_to_all | solution.py:240
  88.1 10.6 %collective-permute-start.4 = (bf16[192,4096]{1,0:T(8,128)(2,1)}, bf16[192,4096]{1,0:T(8,128)(2,1)S(1)}, u32[]{:S(2)}, u32[]{:S(2)}) collective-permute-start(bf16[192,4096]{1,0:T(8,128)(2,1)} %ga_ref.1), channel_id=1, source_target_pairs={{0,16},{16,0},{1,17},{17,1},{2,18},{18,2},{3,19},{19,3},{4,20},{20... | collective-permute-start | bytes 4718600 | tf_op jit(solution)/shard_map/ppermute | solution.py:276
  90.1 11.1 %collective-permute-start.5 = (bf16[192,4096]{1,0:T(8,128)(2,1)}, bf16[192,4096]{1,0:T(8,128)(2,1)S(1)}, u32[]{:S(2)}, u32[]{:S(2)}) collective-permute-start(bf16[192,4096]{1,0:T(8,128)(2,1)} %ua_ref.1), channel_id=1, source_target_pairs={{0,16},{16,0},{1,17},{17,1},{2,18},{18,2},{3,19},{19,3},{4,20},{20... | collective-permute-start | bytes 4718600 | tf_op jit(solution)/shard_map/ppermute | solution.py:276
  92.5 34.9 %collective-permute-start.6 = (bf16[4,1536,128]{2,1,0:T(8,128)(2,1)}, bf16[4,1536,128]{2,1,0:T(8,128)(2,1)}, u32[]{:S(2)}, u32[]{:S(2)}) collective-permute-start(bf16[4,1536,128]{2,1,0:T(8,128)(2,1)} %refs_0_.1), channel_id=1, source_target_pairs={{0,16},{16,0},{1,17},{17,1},{2,18},{18,2},{3,19},{19,3},{4,20},{20... | collective-permute-start | bytes 4718600 | tf_op jit(solution)/shard_map/ppermute | solution.py:276
  94.4 33.0 %collective-permute-start.7 = (bf16[4,1536,128]{2,1,0:T(8,128)(2,1)}, bf16[4,1536,128]{2,1,0:T(8,128)(2,1)}, u32[]{:S(2)}, u32[]{:S(2)}) collective-permute-start(bf16[4,1536,128]{2,1,0:T(8,128)(2,1)} %copy-done.6), channel_id=1, source_target_pairs={{0,16},{16,0},{1,17},{17,1},{2,18},{18,2},{3,19},{19,3},{4,20},{20... | collective-permute-start | bytes 4718600 | tf_op jit(solution)/shard_map/ppermute | solution.py:276
  96.8 30.6 %collective-permute-start.8 = (bf16[4,1536,128]{2,1,0:T(8,128)(2,1)}, bf16[4,1536,128]{2,1,0:T(8,128)(2,1)}, u32[]{:S(2)}, u32[]{:S(2)}) collective-permute-start(bf16[4,1536,128]{2,1,0:T(8,128)(2,1)} %collective-permute-done.3.refs_2_), channel_id=1, source_target_pairs={{0,16},{16,0},{1,17},{17,1},{2,18},{18,2},{3,19},{19,3},{4,20},{20... | collective-permute-start | bytes 4718600 | tf_op jit(solution)/shard_map/ppermute | solution.py:276
  98.8 2.4 %copy-start.4 = (bf16[192,4096]{1,0:T(8,128)(2,1)}, bf16[192,4096]{1,0:T(8,128)(2,1)S(1)}, u32[]{:S(2)}) copy-start(bf16[192,4096]{1,0:T(8,128)(2,1)S(1)} %collective-permute-done.4.gb_ref) | copy-start | bytes 4718596
  98.8 28.6 %collective-permute-start.9 = (bf16[2,1536,128]{2,1,0:T(8,128)(2,1)}, bf16[2,1536,128]{2,1,0:T(8,128)(2,1)S(1)}, u32[]{:S(2)}, u32[]{:S(2)}) collective-permute-start(bf16[2,1536,128]{2,1,0:T(8,128)(2,1)} %collective-permute-done.refs_3_), channel_id=1, source_target_pairs={{0,16},{16,0},{1,17},{17,1},{2,18},{18,2},{3,19},{19,3},{4,20},{20... | collective-permute-start | bytes 2359304 | tf_op jit(solution)/shard_map/ppermute | solution.py:276
  101.2 1.2 copy-start.5
  102.4 25.0 %collective-permute-start.10 = (bf16[2,1536,128]{2,1,0:T(8,128)(2,1)}, bf16[2,1536,128]{2,1,0:T(8,128)(2,1)}, u32[]{:S(2)}, u32[]{:S(2)}) collective-permute-start(bf16[2,1536,128]{2,1,0:T(8,128)(2,1)} %collective-permute-done.1.refs_4_), channel_id=1, source_target_pairs={{0,16},{16,0},{1,17},{17,1},{2,18},{18,2},{3,19},{19,3},{4,20},{20... | collective-permute-start | bytes 2359304 | tf_op jit(solution)/shard_map/ppermute | solution.py:276
  123.5 15.5 %all-to-all-start.4 = ((bf16[16,64,384]{2,1,0:T(8,128)(2,1)}), bf16[16,64,384]{2,1,0:T(8,128)(2,1)S(1)}, u32[]{:S(2)}, u32[]{:S(2)}) async-start(bf16[16,64,384]{2,1,0:T(8,128)(2,1)} %get-tuple-element.22), calls=%async_computation.4 | async-start | bytes 1572864 | tf_op jit(solution)/shard_map/all_to_all | solution.py:240
  127.4 11.6 %copy-start.7 = (bf16[2,1536,128]{2,1,0:T(8,128)(2,1)}, bf16[2,1536,128]{2,1,0:T(8,128)(2,1)S(1)}, u32[]{:S(2)}) copy-start(bf16[2,1536,128]{2,1,0:T(8,128)(2,1)S(1)} %collective-permute-done.9.refs_8_) | copy-start | bytes 2359300

commit v4 on v3

--- a/solution.py
+++ b/solution.py
@@ -109,42 +109,41 @@
             stream_ref[r : r + 1, at] = stream[h : h + 1]
         square = jnp.sum(jnp.sum(stream * stream, axis=1, keepdims=True), axis=0, keepdims=True)
         normed = (stream * lax.rsqrt(square / D + 1e-06) * gain_ref[...]).astype(jnp.bfloat16)
-        for e in range(out_ref.shape[0]):
-            out_ref[e, r * 32 : (r + 1) * 32] = normed
-    for e in range(out_ref.shape[0]):
-        out_ref[e, 64:80] = meta_ref[...]
+        out_ref[r * 32 : (r + 1) * 32] = normed
+    out_ref[64:80] = meta_ref[...]
     attn_ref[...] = line_ref[...].astype(jnp.bfloat16)
 
 
-def select_kernel(expert_ref, rows_ref, meta_ref, out_ref):
+def select_kernel(expert_ref, rows_ref, meta_ref, out_ref, line_ref):
     meta = meta_ref[...].astype(jnp.float32)
     mine = lax.broadcasted_iota(jnp.int32, meta.shape, 1) == expert_ref[0]
     meta = jnp.sum(jnp.where(mine, meta, 0.0), axis=1)
-    line = meta.astype(jnp.bfloat16)
+    line_ref[...] = meta
     first = rows_ref[:, :D].astype(jnp.float32)
     second = rows_ref[:, D:].astype(jnp.float32)
     for x in range(LOCAL):
         pick = meta[:, 16 + x : 17 + x] > 0.5
         row = jnp.where(pick, second, first).astype(jnp.bfloat16)
         for y in range(4):
-            out_ref[x * 4 + y, :, :D] = row
-            out_ref[x * 4 + y, :, D:] = line
-
-
-def up_kernel(
-    core_ref, rows_ref, ga_ref, ua_ref, gb_ref, ub_ref, out_ref, gate_ref, held_ref, sems
-):
+            out_ref[x * 4 + y] = row
+
+
+def expert_kernel(core_ref, rows_ref, *refs):
+    w_refs, (out_ref, held_ref, down_ref, sems) = refs[:6], refs[6:]
     copies = [
-        pltpu.make_async_copy(w_ref, held_ref.at[pl.ds(i * UNITS, UNITS)], sems.at[i])
-        for i, w_ref in enumerate((ga_ref, ua_ref, gb_ref, ub_ref))
+        pltpu.make_async_copy(w_refs[i], held_ref.at[pl.ds(i * UNITS, UNITS)], sems.at[i])
+        for i in range(4)
+    ]
+    copies += [
+        pltpu.make_async_copy(w_refs[4 + i], down_ref.at[i], sems.at[4 + i]) for i in range(2)
     ]
     for copy in copies:
         copy.start()
-    for copy in copies:
+    for copy in copies[:4]:
         copy.wait()
     dims = (((1,), (1,)), ((), ()))
     total = lax.dot_general(
-        rows_ref[:, :D], held_ref[...], dims, preferred_element_type=jnp.float32
+        rows_ref[...], held_ref[...], dims, preferred_element_type=jnp.float32
     )
     parts = [total[:, i * UNITS : (i + 1) * UNITS] for i in range(4)]
     acts = [
@@ -156,76 +155,56 @@
         jnp.concatenate(acts, axis=1),
         jnp.concatenate(acts[::-1], axis=1),
     ).astype(jnp.bfloat16)
-    for x in range(4):
-        for y in range(4):
-            there = slice((x * 4 + y) * 16, (x * 4 + y + 1) * 16)
-            here = slice((x // 2 * 2 + y // 2) * 16, (x // 2 * 2 + y // 2 + 1) * 16)
-            gate_ref[x % 2 * 2 + y % 2, here] = rows_ref[there, D:]
-            for to_x in (x % 2, x % 2 + 2):
-                for to_y in (y % 2, y % 2 + 2):
-                    out_ref[to_x * 4 + to_y, here] = both[there]
-
-
-def down_kernel(place_ref, act_ref, gate_ref, *refs):
-    w_refs, (out_ref, held_ref, sems) = refs[:10], refs[10:]
-    copies = []
+    for copy in copies[4:]:
+        copy.wait()
+    for b in range(16):
+        w = jnp.concatenate([down_ref[0, b], down_ref[1, b]], axis=1)
+        part = jnp.dot(both, w, preferred_element_type=jnp.float32).astype(jnp.bfloat16)
+        for p in range(16):
+            out_ref[p, :, b * 256 : (b + 1) * 256] = part[p * 16 : (p + 1) * 16]
+
+
+def mix_kernel(line_ref, landed_ref, out_ref):
+    row = lax.broadcasted_iota(jnp.int32, (32, 16), 0)
+    slot = lax.broadcasted_iota(jnp.int32, (32, 16), 1)
+    twice = jnp.where(row // 2 == slot, 1.0, 0.0)
+    line = line_ref[...]
+    second = lax.broadcasted_iota(jnp.int32, (32, 1), 0) % 2
+    weights = []
     for x in range(LOCAL):
-        sources = []
-        for c in range(2):
-            own, by_x, by_y, *by_both = w_refs[5 * c : 5 * c + 5]
-            sources += [own.at[x], by_x.at[x], by_y.at[x], by_both[x // 2].at[x % 2]]
-        copies.append(
-            [
-                pltpu.make_async_copy(source, held_ref.at[x, i], sems.at[x, i])
-                for i, source in enumerate(sources)
-            ]
-        )
-        for copy in copies[-1]:
-            copy.start()
-    n = act_ref.shape[1]
-    row = lax.broadcasted_iota(jnp.int32, (2 * n, n), 0)
-    slot = lax.broadcasted_iota(jnp.int32, (2 * n, n), 1)
-    twice = jnp.where(row // 2 == slot, 1.0, 0.0).astype(jnp.bfloat16)
-    gates = gate_ref[place_ref[0] * 2 + place_ref[1]]
-    gates = jnp.dot(twice, gates, preferred_element_type=jnp.float32)
-    lane = lax.broadcasted_iota(jnp.int32, gates.shape, 1)
-    second = lax.broadcasted_iota(jnp.int32, gates.shape, 0) % 2
-    sums = [0.0] * 4
-    for x in range(LOCAL):
-        act = jnp.concatenate([act_ref[x * 4 + y] for y in range(4)], axis=1)
-        act = jnp.dot(twice, act, preferred_element_type=jnp.float32).astype(jnp.bfloat16)
-        at = second * LOCAL + x
-        weight = jnp.sum(
-            jnp.where((lane == at) | (lane == at + 8), gates, 0.0), axis=1, keepdims=True
-        )
-        for copy in copies[x]:
-            copy.wait()
-        for b in range(4):
-            w = jnp.concatenate([held_ref[x, 2 * b], held_ref[x, 2 * b + 1]], axis=1)
-            sums[b] += weight * jnp.dot(act, w, preferred_element_type=jnp.float32)
-    for p in range(out_ref.shape[0]):
-        for b in range(4):
-            part = sums[b][p * 2 : (p + 1) * 2].astype(jnp.bfloat16)
-            out_ref[p, :, b * 256 : (b + 1) * 256] = part
-
-
-def last_kernel(place_ref, landed_ref, stream_ref, out_ref):
-    core = place_ref[2]
-    for g in range(4):
-        total = landed_ref[g * 16].astype(jnp.float32)
-        for z in range(1, 16):
-            total += landed_ref[g * 16 + z].astype(jnp.float32)
-        for b in range(8):
-            of = core if b < 4 else 1 - core
-            x = (g // 2) * 2 + place_ref[0]
-            y = (g % 2) * 2 + place_ref[1]
-            if b & 1:
-                x = lax.rem(x + 1 + 2 * of, 4)
-            if b & 2:
-                y = lax.rem(y + 1 + 2 * of, 4)
-            at = pl.ds(pl.multiple_of(x * 1024 + y * 256 + of * HEAD, HEAD), HEAD)
-            mixture = total[:, b * HEAD : (b + 1) * HEAD]
-            out_ref[:, at] = (stream_ref[:, at] + mixture).astype(jnp.bfloat16)
+        both = []
+        for r in range(2):
+            j = r * LOCAL + x
+            gate = line[:, j : j + 1] + line[:, 8 + j : 9 + j]
+            gate = jnp.sum(jnp.where(row // 2 == slot, gate.reshape(1, 16), 0.0), axis=1)
+            both.append(gate.reshape(32, 1))
+        weights.append(jnp.where(second == 0, both[0], both[1]))
+    twice = twice.astype(jnp.bfloat16)
+    width = 512
+    for k in range(D // width):
+        at = slice(k * width, (k + 1) * width)
+        mixed = 0.0
+        for x in range(LOCAL):
+            total = landed_ref[x * 4, :, at].astype(jnp.float32)
+            for y in range(1, 4):
+                total += landed_ref[x * 4 + y, :, at].astype(jnp.float32)
+            total = jnp.dot(twice, total.astype(jnp.bfloat16), preferred_element_type=jnp.float32)
+            mixed += weights[x] * total
+        for z in range(16):
+            out_ref[z, :, at] = mixed[2 * z : 2 * z + 2].astype(jnp.bfloat16)
+
+
+def last_kernel(core_ref, landed_ref, stream_ref, out_ref):
+    total = landed_ref[0].astype(jnp.float32)
+    for z in range(1, 16):
+        total += landed_ref[z].astype(jnp.float32)
+    even = core_ref[0] == 0
+    for b in range(16):
+        at = slice(b * 256, (b + 1) * 256)
+        mixture = total[:, at]
+        turned = jnp.concatenate([mixture[:, HEAD:], mixture[:, :HEAD]], axis=1)
+        mixture = jnp.where(even, mixture, turned)
+        out_ref[:, at] = (stream_ref[:, at] + mixture).astype(jnp.bfloat16)
 
 
 def in_hbm(a):
@@ -269,7 +248,6 @@
 ):
     bf16, f32 = jnp.bfloat16, jnp.float32
     core = lax.axis_index("c").reshape(1)
-    place = jnp.stack([lax.axis_index(a) for a in ("xl", "yl", "c")])
     expert = lax.axis_index(Z).reshape(1)
     me = lax.axis_index(PLANE).reshape(1)
     owners = 16
@@ -297,10 +275,6 @@
         compiler_params=params(4),
         name="resident_attention",
     )(res_len, mine, res_cache[0])
-    onward = [(i * 2 + c, ((i + 3 + 2 * c) % 4) * 2 + c) for i in range(4) for c in range(2)]
-    far = [
-        (i * 8 + t, (onward[2 * i + t % 2][1] // 2) * 8 + u) for i in range(4) for t, u in onward
-    ]
     source = migrate_from.reshape(32)
     guest = pl.pallas_call(
         guest_kernel,
@@ -317,7 +291,7 @@
         out_shape=(
             jax.ShapeDtypeStruct((2, D), bf16),
             jax.ShapeDtypeStruct((2, D), f32),
-            jax.ShapeDtypeStruct((owners, 80, HEAD), bf16),
+            jax.ShapeDtypeStruct((80, HEAD), bf16),
         ),
         in_specs=[SMEM, SMEM] + [VMEM] * 5,
         out_specs=(VMEM, VMEM, VMEM),
@@ -325,51 +299,44 @@
         compiler_params=params(8),
         name="tokens",
     )(me, source, own, back, resid.reshape(2, HEADS, HEAD), norm_gain.reshape(HEADS, HEAD), meta)
-    later = tie(stream, w_down)
-    by_x = lax.ppermute(later, X + ("c",), onward)
-    by_y = lax.ppermute(later, Y + ("c",), onward)
-    by_both = [lax.ppermute(a, PLANE, far) for a in (later[:2], later[2:])]
-
-    arrived = exchange(tokens, ("zl", "zh"))
-    chosen = pl.pallas_call(
+    down_a = exchange(tie(stream, w_down).reshape(16, 2 * UNITS, HEAD), XY)
+    arrived = lax.all_gather(tokens, Z)
+    chosen, line = pl.pallas_call(
         select_kernel,
-        out_shape=jax.ShapeDtypeStruct((16, owners, D + HEAD), bf16),
+        out_shape=(
+            jax.ShapeDtypeStruct((16, owners, D), bf16),
+            jax.ShapeDtypeStruct((owners, HEAD), f32),
+        ),
         in_specs=[SMEM, VMEM, VMEM],
-        out_specs=VMEM,
+        out_specs=(VMEM, VMEM),
         compiler_params=params(12),
         name="select_rows",
     )(expert, arrived[:, :64].reshape(owners, 2 * D), arrived[:, 64:])
-    chosen, by_both, by_x, by_y = lax.optimization_barrier((chosen, by_both, by_x, by_y))
-    gate_b, up_b = swap(w_gate), swap(w_up)
-    downs = [w_down, by_x, by_y] + by_both
-    downs += [swap(a) for a in downs]
-    chosen = exchange(chosen, XY).reshape(16 * owners, D + HEAD)
-    hidden, gates = pl.pallas_call(
-        up_kernel,
-        out_shape=(
-            jax.ShapeDtypeStruct((16, 64, 2 * UNITS), bf16),
-            jax.ShapeDtypeStruct((4, 64, HEAD), bf16),
-        ),
-        in_specs=[SMEM, VMEM] + [HBM] * 4,
-        out_specs=(VMEM, VMEM),
-        scratch_shapes=[pltpu.VMEM((4 * UNITS, D), bf16), pltpu.SemaphoreType.DMA((4,))],
-        compiler_params=params(20),
-        name="gate_up",
-    )(core, chosen, *[in_hbm(a) for a in (w_gate, w_up, gate_b, up_b)])
-    hidden = exchange(hidden, XY)
-    partial = pl.pallas_call(
-        down_kernel,
-        out_shape=jax.ShapeDtypeStruct((64, 2, 8 * HEAD), bf16),
-        in_specs=[SMEM, VMEM, VMEM] + [HBM] * 10,
+    chosen, down_a = lax.optimization_barrier((chosen, down_a))
+    gate_b, up_b, down_b = swap(w_gate), swap(w_up), swap(down_a)
+    chosen = exchange(chosen, XY).reshape(16 * owners, D)
+    produced = pl.pallas_call(
+        expert_kernel,
+        out_shape=jax.ShapeDtypeStruct((16, owners, D), bf16),
+        in_specs=[SMEM, VMEM] + [HBM] * 6,
         out_specs=VMEM,
         scratch_shapes=[
-            pltpu.VMEM((LOCAL, 8, FFW, HEAD), bf16),
-            pltpu.SemaphoreType.DMA((LOCAL, 8)),
+            pltpu.VMEM((4 * UNITS, D), bf16),
+            pltpu.VMEM((2, 16, 2 * UNITS, HEAD), bf16),
+            pltpu.SemaphoreType.DMA((6,)),
         ],
-        compiler_params=params(24),
-        name="down",
-    )(place, hidden, gates, *[in_hbm(a) for a in downs])
-    landed = exchange(partial, ("xh", "yh", "zl", "zh"))
+        compiler_params=params(28),
+        name="experts",
+    )(core, chosen, *[in_hbm(a) for a in (w_gate, w_up, gate_b, up_b, down_a, down_b)])
+    mixed = pl.pallas_call(
+        mix_kernel,
+        out_shape=jax.ShapeDtypeStruct((owners, 2, D), bf16),
+        in_specs=[VMEM, VMEM],
+        out_specs=VMEM,
+        compiler_params=params(8),
+        name="mix",
+    )(line, exchange(produced, XY))
+    landed = exchange(mixed, Z)
     layer_out = pl.pallas_call(
         last_kernel,
         out_shape=jax.ShapeDtypeStruct((2, D), bf16),
@@ -377,7 +344,7 @@
         out_specs=VMEM,
         compiler_params=params(4),
         name="layer_out",
-    )(place, landed, stream)
+    )(core, landed, stream)
     return attn, layer_out
 
 

time: 182 us -> 171 us (0.940)
  blocking collectives: 35.1 us -> 88.6 us
  starting transfers between devices: 62.2 us -> 28.5 us
  waiting for transfers between devices: 54.1 us -> 29.4 us
  Pallas kernels: 20.9 us -> 14.6 us
    all_gather x0 -> x1, blocking collectives: none -> 35 us  [on_device(): arrived = lax.all_gather(tokens, Z)]
    all_to_all x5 -> x4, waiting for transfers between devices: 52.6 us -> 26.7 us  [exchange(): return lax.all_to_all(a, axes, split_axis=0, concat_axis=0, tiled=True)]
    all_to_all x1 -> x2, blocking collectives: 35.1 us -> 53.6 us  [exchange(): return lax.all_to_all(a, axes, split_axis=0, concat_axis=0, tiled=True)]
    all_to_all x5 -> x4, starting transfers between devices: 34.8 us -> 22.2 us  [exchange(): return lax.all_to_all(a, axes, split_axis=0, concat_axis=0, tiled=True)]
    ppermute x4 -> x0, starting transfers between devices: 12.5 us -> none  [the longest x2 6.46 us: on_device(): by_both = [lax.ppermute(a, PLANE, far) for a in (later[:2], later[2:])]]
    ppermute x7 -> x3, starting transfers between devices: 14.9 us -> 6.25 us  [on_device(): swap = lambda a: lax.ppermute(a, 'c', [(0, 1), (1, 0)])]
    pallas_call x3, Pallas kernels: 13.5 us -> 7.97 us  [the longest x1 7.17 us: on_device(): pl.pallas_call(expert_kernel, out_shape=jax.ShapeDtypeStruct((16, owners,...]
    ppermute x7 -> x3, waiting for transfers between devices: 0.02 us -> 2.69 us  [on_device(): swap = lambda a: lax.ppermute(a, 'c', [(0, 1), (1, 0)])]
  transfers between devices with their start and end apart: 16 -> 7, of which waited for: 6 -> 5; matrix products, arithmetic and copies ran while one was open for 2% -> 2% of each run, Pallas kernels for 4% -> 0%
where the time goes in v4:
time: 171 us; the launch traced here: 170 us
  blocking collectives  88.6 us (52%)
  waiting for transfers between devices  29.4 us (17%)
  starting transfers between devices  28.5 us (17%)
  Pallas kernels  14.6 us (9%)
  local copies, waits for them, and re-layouts  5.76 us (3%)
    all_to_all x2, blocking collectives, exchange(): return lax.all_to_all(a, axes, split_axis=0, concat_axis=0, tiled=True)  53.6 us
    all_gather x1, blocking collectives, on_device(): arrived = lax.all_gather(tokens, Z)  35 us
    all_to_all x4, waiting for transfers between devices, exchange(): return lax.all_to_all(a, axes, split_axis=0, concat_axis=0, tiled=True)  26.7 us
    all_to_all x4, starting transfers between devices, exchange(): return lax.all_to_all(a, axes, split_axis=0, concat_axis=0, tiled=True)  22.2 us
    pallas_call x1, Pallas kernels, on_device(): pl.pallas_call(expert_kernel, out_shape=jax.ShapeDtypeStruct((16, owners,...  7.17 us
    ppermute x3, starting transfers between devices, on_device(): swap = lambda a: lax.ppermute(a, 'c', [(0, 1), (1, 0)])  6.25 us
    unnamed x16, local copies, waits for them, and re-layouts  5.48 us
  transfers between devices with their start and end apart: 7, of which 5 were waited for; matrix products, arithmetic and copies ran while one was open for 2% of the time, Pallas kernels for 0%

profile of v4, /device:TPU:32, one launch (start us, length us, event | category | flops | bytes accessed | tf_op | source)
XLA Modules:
  0.0 169.9 jit_solution(11728010562305084494)
XLA Ops:
  0.6 0.0 copy-start.3
  0.6 0.0 copy-start.2
  0.7 1.5 ask.1
  2.2 7.3 %all-to-all-start = ((bf16[32,48,128]{2,1,0:T(8,128)(2,1)}), bf16[32,48,128]{2,1,0:T(8,128)(2,1)S(1)}, u32[]{:S(2)}, u32[]{:S(2)}) async-start(bf16[32,48,128]{2,1,0:T(8,128)(2,1)} %get-tuple-element.13), calls=%async_computation | async-start | bytes 786432 | tf_op jit(solution)/shard_map/all_to_all | solution.py:219
  9.5 0.8 select_reduce_fusion
  10.3 0.1 copy.22
  11.0 0.1 copy.23
  11.1 0.8 broadcast_compare_fusion
  11.9 0.1 copy.24
  12.0 0.7 copy.30
  12.7 0.0 copy-start.1
  12.7 0.9 copy-done.1
  13.6 0.6 resident_attention.1.own_ref
  14.2 5.2 %all-to-all-done.asked_ref = bf16[32,48,128]{2,1,0:T(8,128)(2,1)S(1)} async-done(((bf16[32,48,128]{2,1,0:T(8,128)(2,1)}), bf16[32,48,128]{2,1,0:T(8,128)(2,1)S(1)}, u32[]{:S(2)}, u32[]{:S(2)}) %all-to-all-start) | async-done | bytes 393248 | tf_op jit(solution)/shard_map/all_to_all | solution.py:219
  19.5 2.6 %guest_attention.1 = bf16[32,32,128]{2,1,0:T(8,128)(2,1)} custom-call(s32[1]{0:T(128)} %bitcast.me_ref, s32[32]{0:T(128)} %bitcast.25, s32[32]{0:T(128)} %bitcast.34, bf16[32,48,128]{2,1,0:T(8,128)(2,1)S(1)} %all-to-all-done.asked_ref, bf16[256,512]{1,0:T(8,128)(2,1)} %bitcast.30), custom_call_target="tpu_custom_call" | custom-call | tf_op jit(solution)/shard_map/guest_attention/pallas_call | solution.py:279
  22.1 3.9 %all-to-all-start.1 = ((bf16[32,32,128]{2,1,0:T(8,128)(2,1)}), bf16[32,32,128]{2,1,0:T(8,128)(2,1)S(1)}, u32[]{:S(2)}, u32[]{:S(2)}) async-start(bf16[32,32,128]{2,1,0:T(8,128)(2,1)} %guest_attention.1), calls=%async_computation.1 | async-start | bytes 524288 | tf_op jit(solution)/shard_map/all_to_all | solution.py:219
  26.0 0.1 fusion.4.meta_ref
  26.1 8.8 %all-to-all-done.1.back_ref = bf16[32,32,128]{2,1,0:T(8,128)(2,1)S(1)} async-done(((bf16[32,32,128]{2,1,0:T(8,128)(2,1)}), bf16[32,32,128]{2,1,0:T(8,128)(2,1)S(1)}, u32[]{:S(2)}, u32[]{:S(2)}) %all-to-all-start.1) | async-done | bytes 262176 | tf_op jit(solution)/shard_map/all_to_all | solution.py:219
  34.9 0.0 copy-done.3
  34.9 0.0 copy-done.2
  34.9 1.2 tokens.1
  36.1 3.7 %all-to-all-start.2 = ((bf16[16,384,128]{2,1,0:T(8,128)(2,1)}), bf16[16,384,128]{2,1,0:T(8,128)(2,1)S(1)}, u32[]{:S(2)}, u32[]{:S(2)}) async-start(bf16[16,384,128]{2,1,0:T(8,128)(2,1)} %bitcast.10), calls=%async_computation.2 | async-start | bytes 3145728 | tf_op jit(solution)/shard_map/all_to_all | solution.py:219
  39.8 35.0 %all-gather = bf16[1280,128]{1,0:T(8,128)(2,1)S(1)} all-gather(bf16[80,128]{1,0:T(8,128)(2,1)S(1)} %get-tuple-element.15), channel_id=2, replica_groups=mesh['xh'=2,'xl'=2,'yh'=2,'yl'=2,'c'=2,'zh'=4,'zl'=4] {'zh','zl'}, dimensions={0}, use_global_device_ids=true | all-gather | bytes 348160 | tf_op jit(solution)/shard_map/all_gather | solution.py:303
  74.9 0.2 copy.29
  75.1 0.3 select_rows.1
  75.3 0.0 copy-start
  75.3 1.3 copy-done
  76.7 0.0 all-to-all-done.2.refs_4_
  76.7 0.0 copy-start.4
  76.7 1.2 copy-done.4
  77.8 7.3 %all-to-all-start.3 = ((bf16[16,16,4096]{2,1,0:T(8,128)(2,1)}), bf16[16,16,4096]{2,1,0:T(8,128)(2,1)S(1)}, u32[]{:S(2)}, u32[]{:S(2)}) async-start(bf16[16,16,4096]{2,1,0:T(8,128)(2,1)} %copy-done), calls=%async_computation.3 | async-start | bytes 4194304 | tf_op jit(solution)/shard_map/all_to_all | solution.py:219
  85.2 1.9 %collective-permute-start = (bf16[192,4096]{1,0:T(8,128)(2,1)}, bf16[192,4096]{1,0:T(8,128)(2,1)S(1)}, u32[]{:S(2)}, u32[]{:S(2)}) collective-permute-start(bf16[192,4096]{1,0:T(8,128)(2,1)} %refs_0_.1), channel_id=1, source_target_pairs={{0,16},{16,0},{1,17},{17,1},{2,18},{18,2},{3,19},{19,3},{4,20},{20... | collective-permute-start | bytes 4718600 | tf_op jit(solution)/shard_map/ppermute | solution.py:254
  87.1 2.4 %collective-permute-start.1 = (bf16[192,4096]{1,0:T(8,128)(2,1)}, bf16[192,4096]{1,0:T(8,128)(2,1)S(1)}, u32[]{:S(2)}, u32[]{:S(2)}) collective-permute-start(bf16[192,4096]{1,0:T(8,128)(2,1)} %refs_1_.1), channel_id=1, source_target_pairs={{0,16},{16,0},{1,17},{17,1},{2,18},{18,2},{3,19},{19,3},{4,20},{20... | collective-permute-start | bytes 4718600 | tf_op jit(solution)/shard_map/ppermute | solution.py:254
  89.5 1.9 %collective-permute-start.2 = (bf16[16,384,128]{2,1,0:T(8,128)(2,1)}, bf16[16,384,128]{2,1,0:T(8,128)(2,1)}, u32[]{:S(2)}, u32[]{:S(2)}) collective-permute-start(bf16[16,384,128]{2,1,0:T(8,128)(2,1)} %copy-done.4), channel_id=1, source_target_pairs={{0,16},{16,0},{1,17},{17,1},{2,18},{18,2},{3,19},{19,3},{4,20},{20... | collective-permute-start | bytes 4718600 | tf_op jit(solution)/shard_map/ppermute | solution.py:254
  91.5 0.0 collective-permute-done.refs_2_
  91.5 0.0 copy-start.5
  91.5 1.5 collective-permute-done.1.refs_3_
  92.9 0.0 copy-done.5
  92.9 0.0 copy-start.6
  93.0 1.2 copy-done.6
  94.1 1.2 collective-permute-done.2.refs_5_
  95.3 12.6 %all-to-all-done.3 = bf16[16,16,4096]{2,1,0:T(8,128)(2,1)S(1)} async-done(((bf16[16,16,4096]{2,1,0:T(8,128)(2,1)}), bf16[16,16,4096]{2,1,0:T(8,128)(2,1)S(1)}, u32[]{:S(2)}, u32[]{:S(2)}) %all-to-all-start.3) | async-done | bytes 2097184 | tf_op jit(solution)/shard_map/all_to_all | solution.py:219
  107.9 7.2 %experts.1 = bf16[16,16,4096]{2,1,0:T(8,128)(2,1)S(1)} custom-call(s32[1]{0:T(128)} %bitcast.7.core_ref, bf16[256,4096]{1,0:T(8,128)(2,1)S(1)} %bitcast.20, bf16[192,4096]{1,0:T(8,128)(2,1)} %refs_0_.1, bf16[192,4096]{1,0:T(8,128)(2,1)} %refs_1_.1, bf16[192,4096]{1,0:T(8,128)(2,1)} %copy-done.5, bf16[192,4096]{1,0:T(8,128)(2,1)} %copy-done.6, ...), custom_call_target="tpu_custom_call" | custom-call | tf_op jit(solution)/shard_map/experts/pallas_call | solution.py:318
  115.1 26.9 %all_to_all.30.landed_ref = bf16[16,16,4096]{2,1,0:T(8,128)(2,1)S(1)} all-to-all(bf16[16,16,4096]{2,1,0:T(8,128)(2,1)S(1)} %experts.1), channel_id=1, replica_groups=mesh['xh'=2,'xl'=2,'yh'=2,'yl'=2,'c'=2,'zh'=4,'zl'=4] {'xh','xl','yh','yl'}, dimensions={0} | all-to-all | bytes 4194304 | tf_op jit(solution)/shard_map/all_to_all | solution.py:219
  142.0 0.5 mix.1
  142.6 26.7 %all_to_all.31.landed_ref = bf16[16,2,4096]{2,1,0:T(2,128)(2,1)S(1)} all-to-all(bf16[16,2,4096]{2,1,0:T(2,128)(2,1)S(1)} %mix.1), channel_id=1, replica_groups=mesh['xh'=2,'xl'=2,'yh'=2,'yl'=2,'c'=2,'zh'=4,'zl'=4] {'zh','zl'}, dimensions={0} | all-to-all | bytes 524288 | tf_op jit(solution)/shard_map/all_to_all | solution.py:219
  169.2 0.7 layer_out.1
  (7 shorter events, 0.1 us)
Async XLA Ops:
  0.6 34.3 %copy-start.3 = (s32[32,1]{0,1:T(1,128)S(1)}, s32[32,1]{0,1:T(1,128)}, u32[]{:S(2)}) copy-start(s32[32,1]{0,1:T(1,128)} %param.22) | copy-start | bytes 388
  0.6 34.3 %copy-start.2 = (f32[4096]{0:T(1024)S(1)}, f32[4096]{0:T(1024)}, u32[]{:S(2)}) copy-start(f32[4096]{0:T(1024)} %param.17) | copy-start | bytes 49156
  2.2 17.3 %all-to-all-start = ((bf16[32,48,128]{2,1,0:T(8,128)(2,1)}), bf16[32,48,128]{2,1,0:T(8,128)(2,1)S(1)}, u32[]{:S(2)}, u32[]{:S(2)}) async-start(bf16[32,48,128]{2,1,0:T(8,128)(2,1)} %get-tuple-element.13), calls=%async_computation | async-start | bytes 786432 | tf_op jit(solution)/shard_map/all_to_all | solution.py:219
  12.7 0.9 copy-start.1
  22.1 12.8 %all-to-all-start.1 = ((bf16[32,32,128]{2,1,0:T(8,128)(2,1)}), bf16[32,32,128]{2,1,0:T(8,128)(2,1)S(1)}, u32[]{:S(2)}, u32[]{:S(2)}) async-start(bf16[32,32,128]{2,1,0:T(8,128)(2,1)} %guest_attention.1), calls=%async_computation.1 | async-start | bytes 524288 | tf_op jit(solution)/shard_map/all_to_all | solution.py:219
  36.1 40.6 %all-to-all-start.2 = ((bf16[16,384,128]{2,1,0:T(8,128)(2,1)}), bf16[16,384,128]{2,1,0:T(8,128)(2,1)S(1)}, u32[]{:S(2)}, u32[]{:S(2)}) async-start(bf16[16,384,128]{2,1,0:T(8,128)(2,1)} %bitcast.10), calls=%async_computation.2 | async-start | bytes 3145728 | tf_op jit(solution)/shard_map/all_to_all | solution.py:219
  75.3 1.3 copy-start
  76.7 1.2 copy-start.4
  77.8 30.1 %all-to-all-start.3 = ((bf16[16,16,4096]{2,1,0:T(8,128)(2,1)}), bf16[16,16,4096]{2,1,0:T(8,128)(2,1)S(1)}, u32[]{:S(2)}, u32[]{:S(2)}) async-start(bf16[16,16,4096]{2,1,0:T(8,128)(2,1)} %copy-done), calls=%async_computation.3 | async-start | bytes 4194304 | tf_op jit(solution)/shard_map/all_to_all | solution.py:219
  85.2 6.3 %collective-permute-start = (bf16[192,4096]{1,0:T(8,128)(2,1)}, bf16[192,4096]{1,0:T(8,128)(2,1)S(1)}, u32[]{:S(2)}, u32[]{:S(2)}) collective-permute-start(bf16[192,4096]{1,0:T(8,128)(2,1)} %refs_0_.1), channel_id=1, source_target_pairs={{0,16},{16,0},{1,17},{17,1},{2,18},{18,2},{3,19},{19,3},{4,20},{20... | collective-permute-start | bytes 4718600 | tf_op jit(solution)/shard_map/ppermute | solution.py:254
  87.1 5.8 %collective-permute-start.1 = (bf16[192,4096]{1,0:T(8,128)(2,1)}, bf16[192,4096]{1,0:T(8,128)(2,1)S(1)}, u32[]{:S(2)}, u32[]{:S(2)}) collective-permute-start(bf16[192,4096]{1,0:T(8,128)(2,1)} %refs_1_.1), channel_id=1, source_target_pairs={{0,16},{16,0},{1,17},{17,1},{2,18},{18,2},{3,19},{19,3},{4,20},{20... | collective-permute-start | bytes 4718600 | tf_op jit(solution)/shard_map/ppermute | solution.py:254
  89.5 5.8 %collective-permute-start.2 = (bf16[16,384,128]{2,1,0:T(8,128)(2,1)}, bf16[16,384,128]{2,1,0:T(8,128)(2,1)}, u32[]{:S(2)}, u32[]{:S(2)}) collective-permute-start(bf16[16,384,128]{2,1,0:T(8,128)(2,1)} %copy-done.4), channel_id=1, source_target_pairs={{0,16},{16,0},{1,17},{17,1},{2,18},{18,2},{3,19},{19,3},{4,20},{20... | collective-permute-start | bytes 4718600 | tf_op jit(solution)/shard_map/ppermute | solution.py:254
  91.5 1.5 copy-start.5
  92.9 1.2 copy-start.6

commit v5 on v4

--- a/solution.py
+++ b/solution.py
@@ -75,7 +75,8 @@
         ask_ref[p] = ask
 
 
-def resident_kernel(len_ref, own_ref, cache_ref, out_ref):
+def resident_kernel(len_ref, own_ref, cache_ref, long_ref, out_ref, held_ref):
+    held_ref[...] = long_ref[...]
     own = own_ref[...]
     out = attend(own[:32], cache_ref, own[32:48][:4], len_ref[0])
     out_ref[...] = out.astype(jnp.bfloat16)
@@ -125,7 +126,7 @@
         pick = meta[:, 16 + x : 17 + x] > 0.5
         row = jnp.where(pick, second, first).astype(jnp.bfloat16)
         for y in range(4):
-            out_ref[x * 4 + y] = row
+            out_ref[y * 4 + x] = row
 
 
 def expert_kernel(core_ref, rows_ref, *refs):
@@ -185,9 +186,9 @@
         at = slice(k * width, (k + 1) * width)
         mixed = 0.0
         for x in range(LOCAL):
-            total = landed_ref[x * 4, :, at].astype(jnp.float32)
+            total = landed_ref[x, :, at].astype(jnp.float32)
             for y in range(1, 4):
-                total += landed_ref[x * 4 + y, :, at].astype(jnp.float32)
+                total += landed_ref[y * 4 + x, :, at].astype(jnp.float32)
             total = jnp.dot(twice, total.astype(jnp.bfloat16), preferred_element_type=jnp.float32)
             mixed += weights[x] * total
         for z in range(16):
@@ -267,14 +268,17 @@
     )(in_hbm(queries), in_hbm(fresh_key_value))
     asked = exchange(ask, PLANE)
 
-    own = pl.pallas_call(
+    own, held_cache = pl.pallas_call(
         resident_kernel,
-        out_shape=jax.ShapeDtypeStruct((HEADS, HEAD), bf16),
-        in_specs=[SMEM, VMEM, VMEM],
-        out_specs=VMEM,
+        out_shape=(
+            jax.ShapeDtypeStruct((HEADS, HEAD), bf16),
+            jax.ShapeDtypeStruct(long_cache.shape[1:], bf16),
+        ),
+        in_specs=[SMEM, VMEM, VMEM, VMEM],
+        out_specs=(VMEM, VMEM),
         compiler_params=params(4),
         name="resident_attention",
-    )(res_len, mine, res_cache[0])
+    )(res_len, mine, res_cache[0], in_hbm(long_cache[0]))
     source = migrate_from.reshape(32)
     guest = pl.pallas_call(
         guest_kernel,
@@ -283,7 +287,7 @@
         out_specs=VMEM,
         compiler_params=params(8),
         name="guest_attention",
-    )(me, in_hbm(source), in_hbm(long_len.reshape(32)), asked, in_hbm(long_cache[0]))
+    )(me, in_hbm(source), in_hbm(long_len.reshape(32)), asked, held_cache)
     back = exchange(guest, PLANE)
     meta = pick_table(expert_ids, gate_wts, owners)
     attn, stream, tokens = pl.pallas_call(
@@ -314,7 +318,7 @@
     )(expert, arrived[:, :64].reshape(owners, 2 * D), arrived[:, 64:])
     chosen, down_a = lax.optimization_barrier((chosen, down_a))
     gate_b, up_b, down_b = swap(w_gate), swap(w_up), swap(down_a)
-    chosen = exchange(chosen, XY).reshape(16 * owners, D)
+    chosen = exchange(chosen, Y + X).reshape(16 * owners, D)
     produced = pl.pallas_call(
         expert_kernel,
         out_shape=jax.ShapeDtypeStruct((16, owners, D), bf16),
@@ -335,7 +339,7 @@
         out_specs=VMEM,
         compiler_params=params(8),
         name="mix",
-    )(line, exchange(produced, XY))
+    )(line, exchange(produced, Y + X))
     landed = exchange(mixed, Z)
     layer_out = pl.pallas_call(
         last_kernel,

time: 171 us -> 169 us (0.988)
  blocking collectives: 88.6 us -> 84.9 us
    all_to_all x2, blocking collectives: 53.6 us -> 49.9 us  [exchange(): return lax.all_to_all(a, axes, split_axis=0, concat_axis=0, tiled=True)]
  transfers between devices with their start and end apart: 7 -> 7, of which waited for: 5 -> 5; matrix products, arithmetic and copies ran while one was open for 2% -> 2% of each run, Pallas kernels for 0% -> 1%
where the time goes in v5:
time: 169 us
  blocking collectives  84.9 us (50%)
  waiting for transfers between devices  31.1 us (18%)
  starting transfers between devices  28.5 us (17%)
  Pallas kernels  15.2 us (9%)
  local copies, waits for them, and re-layouts  5.75 us (3%)
    all_to_all x2, blocking collectives, exchange(): return lax.all_to_all(a, axes, split_axis=0, concat_axis=0, tiled=True)  49.9 us
    all_gather x1, blocking collectives, on_device(): arrived = lax.all_gather(tokens, Z)  35 us
    all_to_all x4, waiting for transfers between devices, exchange(): return lax.all_to_all(a, axes, split_axis=0, concat_axis=0, tiled=True)  28.4 us
    all_to_all x4, starting transfers between devices, exchange(): return lax.all_to_all(a, axes, split_axis=0, concat_axis=0, tiled=True)  22.2 us
    pallas_call x1, Pallas kernels, on_device(): pl.pallas_call(expert_kernel, out_shape=jax.ShapeDtypeStruct((16, owners,...  7.17 us
    ppermute x3, starting transfers between devices, on_device(): swap = lambda a: lax.ppermute(a, 'c', [(0, 1), (1, 0)])  6.25 us
    unnamed x16, local copies, waits for them, and re-layouts  5.47 us
  transfers between devices with their start and end apart: 7, of which 5 were waited for; matrix products, arithmetic and copies ran while one was open for 2% of the time, Pallas kernels for 1%

profile of v5, /device:TPU:32, one launch (start us, length us, event | category | flops | bytes accessed | tf_op | source)
XLA Modules:
  0.0 168.6 jit_solution(1878451849521726968)
XLA Ops:
  0.6 0.0 copy-start.3
  0.6 0.0 copy-start.2
  0.7 1.5 ask.1
  2.2 7.3 %all-to-all-start = ((bf16[32,48,128]{2,1,0:T(8,128)(2,1)}), bf16[32,48,128]{2,1,0:T(8,128)(2,1)S(1)}, u32[]{:S(2)}, u32[]{:S(2)}) async-start(bf16[32,48,128]{2,1,0:T(8,128)(2,1)} %get-tuple-element.16), calls=%async_computation | async-start | bytes 786432 | tf_op jit(solution)/shard_map/all_to_all | solution.py:220
  9.5 0.8 select_reduce_fusion
  10.3 0.1 copy.22
  11.1 0.1 copy.23
  11.1 0.8 broadcast_compare_fusion
  11.9 0.1 copy.24
  12.0 0.7 copy.30
  12.8 0.0 copy-start.1
  12.8 0.9 copy-done.1
  13.7 1.5 resident_attention.1
  15.2 4.3 %all-to-all-done.asked_ref = bf16[32,48,128]{2,1,0:T(8,128)(2,1)S(1)} async-done(((bf16[32,48,128]{2,1,0:T(8,128)(2,1)}), bf16[32,48,128]{2,1,0:T(8,128)(2,1)S(1)}, u32[]{:S(2)}, u32[]{:S(2)}) %all-to-all-start) | async-done | bytes 393248 | tf_op jit(solution)/shard_map/all_to_all | solution.py:220
  19.5 2.3 %guest_attention.1 = bf16[32,32,128]{2,1,0:T(8,128)(2,1)} custom-call(s32[1]{0:T(128)} %bitcast.me_ref, s32[32]{0:T(128)} %bitcast.25, s32[32]{0:T(128)} %bitcast.34, bf16[32,48,128]{2,1,0:T(8,128)(2,1)S(1)} %all-to-all-done.asked_ref, bf16[256,512]{1,0:T(8,128)(2,1)S(1)} %get-tuple-element.17.cache_ref), custom_call_target="tpu_custom_call" | custom-call | tf_op jit(solution)/shard_map/guest_attention/pallas_call | solution.py:283
  21.8 3.9 %all-to-all-start.1 = ((bf16[32,32,128]{2,1,0:T(8,128)(2,1)}), bf16[32,32,128]{2,1,0:T(8,128)(2,1)S(1)}, u32[]{:S(2)}, u32[]{:S(2)}) async-start(bf16[32,32,128]{2,1,0:T(8,128)(2,1)} %guest_attention.1), calls=%async_computation.1 | async-start | bytes 524288 | tf_op jit(solution)/shard_map/all_to_all | solution.py:220
  25.7 0.1 fusion.4.meta_ref
  25.8 8.8 %all-to-all-done.1.back_ref = bf16[32,32,128]{2,1,0:T(8,128)(2,1)S(1)} async-done(((bf16[32,32,128]{2,1,0:T(8,128)(2,1)}), bf16[32,32,128]{2,1,0:T(8,128)(2,1)S(1)}, u32[]{:S(2)}, u32[]{:S(2)}) %all-to-all-start.1) | async-done | bytes 262176 | tf_op jit(solution)/shard_map/all_to_all | solution.py:220
  34.6 0.0 copy-done.3
  34.6 0.0 copy-done.2
  34.6 1.2 tokens.1
  35.8 3.7 %all-to-all-start.2 = ((bf16[16,384,128]{2,1,0:T(8,128)(2,1)}), bf16[16,384,128]{2,1,0:T(8,128)(2,1)S(1)}, u32[]{:S(2)}, u32[]{:S(2)}) async-start(bf16[16,384,128]{2,1,0:T(8,128)(2,1)} %bitcast.10), calls=%async_computation.2 | async-start | bytes 3145728 | tf_op jit(solution)/shard_map/all_to_all | solution.py:220
  39.5 35.0 %all-gather = bf16[1280,128]{1,0:T(8,128)(2,1)S(1)} all-gather(bf16[80,128]{1,0:T(8,128)(2,1)S(1)} %get-tuple-element.19), channel_id=2, replica_groups=mesh['xh'=2,'xl'=2,'yh'=2,'yl'=2,'c'=2,'zh'=4,'zl'=4] {'zh','zl'}, dimensions={0}, use_global_device_ids=true | all-gather | bytes 348160 | tf_op jit(solution)/shard_map/all_gather | solution.py:307
  74.6 0.2 copy.29
  74.8 0.3 select_rows.1
  75.0 0.0 copy-start
  75.1 1.3 copy-done
  76.4 0.0 all-to-all-done.2.refs_4_
  76.4 0.0 copy-start.4
  76.4 1.2 copy-done.4
  77.6 7.3 %all-to-all-start.3 = ((bf16[16,16,4096]{2,1,0:T(8,128)(2,1)}), bf16[16,16,4096]{2,1,0:T(8,128)(2,1)S(1)}, u32[]{:S(2)}, u32[]{:S(2)}) async-start(bf16[16,16,4096]{2,1,0:T(8,128)(2,1)} %copy-done), calls=%async_computation.3 | async-start | bytes 4194304 | tf_op jit(solution)/shard_map/all_to_all | solution.py:220
  84.9 1.9 %collective-permute-start = (bf16[192,4096]{1,0:T(8,128)(2,1)}, bf16[192,4096]{1,0:T(8,128)(2,1)S(1)}, u32[]{:S(2)}, u32[]{:S(2)}) collective-permute-start(bf16[192,4096]{1,0:T(8,128)(2,1)} %refs_0_.1), channel_id=1, source_target_pairs={{0,16},{16,0},{1,17},{17,1},{2,18},{18,2},{3,19},{19,3},{4,20},{20... | collective-permute-start | bytes 4718600 | tf_op jit(solution)/shard_map/ppermute | solution.py:255
  86.8 2.4 %collective-permute-start.1 = (bf16[192,4096]{1,0:T(8,128)(2,1)}, bf16[192,4096]{1,0:T(8,128)(2,1)S(1)}, u32[]{:S(2)}, u32[]{:S(2)}) collective-permute-start(bf16[192,4096]{1,0:T(8,128)(2,1)} %refs_1_.1), channel_id=1, source_target_pairs={{0,16},{16,0},{1,17},{17,1},{2,18},{18,2},{3,19},{19,3},{4,20},{20... | collective-permute-start | bytes 4718600 | tf_op jit(solution)/shard_map/ppermute | solution.py:255
  89.2 1.9 %collective-permute-start.2 = (bf16[16,384,128]{2,1,0:T(8,128)(2,1)}, bf16[16,384,128]{2,1,0:T(8,128)(2,1)}, u32[]{:S(2)}, u32[]{:S(2)}) collective-permute-start(bf16[16,384,128]{2,1,0:T(8,128)(2,1)} %copy-done.4), channel_id=1, source_target_pairs={{0,16},{16,0},{1,17},{17,1},{2,18},{18,2},{3,19},{19,3},{4,20},{20... | collective-permute-start | bytes 4718600 | tf_op jit(solution)/shard_map/ppermute | solution.py:255
  91.2 0.0 collective-permute-done.refs_2_
  91.2 0.0 copy-start.5
  91.2 1.5 collective-permute-done.1.refs_3_
  92.7 0.0 copy-done.5
  92.7 0.0 copy-start.6
  92.7 1.2 copy-done.6
  93.8 1.2 collective-permute-done.2.refs_5_
  95.0 15.2 %all-to-all-done.3 = bf16[16,16,4096]{2,1,0:T(8,128)(2,1)S(1)} async-done(((bf16[16,16,4096]{2,1,0:T(8,128)(2,1)}), bf16[16,16,4096]{2,1,0:T(8,128)(2,1)S(1)}, u32[]{:S(2)}, u32[]{:S(2)}) %all-to-all-start.3) | async-done | bytes 2097184 | tf_op jit(solution)/shard_map/all_to_all | solution.py:220
  110.3 7.2 %experts.1 = bf16[16,16,4096]{2,1,0:T(8,128)(2,1)S(1)} custom-call(s32[1]{0:T(128)} %bitcast.7.core_ref, bf16[256,4096]{1,0:T(8,128)(2,1)S(1)} %bitcast.20, bf16[192,4096]{1,0:T(8,128)(2,1)} %refs_0_.1, bf16[192,4096]{1,0:T(8,128)(2,1)} %refs_1_.1, bf16[192,4096]{1,0:T(8,128)(2,1)} %copy-done.5, bf16[192,4096]{1,0:T(8,128)(2,1)} %copy-done.6, ...), custom_call_target="tpu_custom_call" | custom-call | tf_op jit(solution)/shard_map/experts/pallas_call | solution.py:322
  117.5 26.1 %all_to_all.30.landed_ref = bf16[16,16,4096]{2,1,0:T(8,128)(2,1)S(1)} all-to-all(bf16[16,16,4096]{2,1,0:T(8,128)(2,1)S(1)} %experts.1), channel_id=1, replica_groups=mesh['xh'=2,'xl'=2,'yh'=2,'yl'=2,'c'=2,'zh'=4,'zl'=4] {'yh','yl','xh','xl'}, dimensions={0} | all-to-all | bytes 4194304 | tf_op jit(solution)/shard_map/all_to_all | solution.py:220
  143.6 0.5 mix.1
  144.1 23.7 %all_to_all.31.landed_ref = bf16[16,2,4096]{2,1,0:T(2,128)(2,1)S(1)} all-to-all(bf16[16,2,4096]{2,1,0:T(2,128)(2,1)S(1)} %mix.1), channel_id=1, replica_groups=mesh['xh'=2,'xl'=2,'yh'=2,'yl'=2,'c'=2,'zh'=4,'zl'=4] {'zh','zl'}, dimensions={0} | all-to-all | bytes 524288 | tf_op jit(solution)/shard_map/all_to_all | solution.py:220
  167.9 0.7 layer_out.1
  (7 shorter events, 0.1 us)
Async XLA Ops:
  0.6 34.0 %copy-start.3 = (s32[32,1]{0,1:T(1,128)S(1)}, s32[32,1]{0,1:T(1,128)}, u32[]{:S(2)}) copy-start(s32[32,1]{0,1:T(1,128)} %param.22) | copy-start | bytes 388
  0.6 34.0 %copy-start.2 = (f32[4096]{0:T(1024)S(1)}, f32[4096]{0:T(1024)}, u32[]{:S(2)}) copy-start(f32[4096]{0:T(1024)} %param.17) | copy-start | bytes 49156
  2.2 17.3 %all-to-all-start = ((bf16[32,48,128]{2,1,0:T(8,128)(2,1)}), bf16[32,48,128]{2,1,0:T(8,128)(2,1)S(1)}, u32[]{:S(2)}, u32[]{:S(2)}) async-start(bf16[32,48,128]{2,1,0:T(8,128)(2,1)} %get-tuple-element.16), calls=%async_computation | async-start | bytes 786432 | tf_op jit(solution)/shard_map/all_to_all | solution.py:220
  12.8 0.9 copy-start.1
  21.8 12.8 %all-to-all-start.1 = ((bf16[32,32,128]{2,1,0:T(8,128)(2,1)}), bf16[32,32,128]{2,1,0:T(8,128)(2,1)S(1)}, u32[]{:S(2)}, u32[]{:S(2)}) async-start(bf16[32,32,128]{2,1,0:T(8,128)(2,1)} %guest_attention.1), calls=%async_computation.1 | async-start | bytes 524288 | tf_op jit(solution)/shard_map/all_to_all | solution.py:220
  35.8 40.6 %all-to-all-start.2 = ((bf16[16,384,128]{2,1,0:T(8,128)(2,1)}), bf16[16,384,128]{2,1,0:T(8,128)(2,1)S(1)}, u32[]{:S(2)}, u32[]{:S(2)}) async-start(bf16[16,384,128]{2,1,0:T(8,128)(2,1)} %bitcast.10), calls=%async_computation.2 | async-start | bytes 3145728 | tf_op jit(solution)/shard_map/all_to_all | solution.py:220
  75.0 1.3 copy-start
  76.4 1.2 copy-start.4
  77.6 32.7 %all-to-all-start.3 = ((bf16[16,16,4096]{2,1,0:T(8,128)(2,1)}), bf16[16,16,4096]{2,1,0:T(8,128)(2,1)S(1)}, u32[]{:S(2)}, u32[]{:S(2)}) async-start(bf16[16,16,4096]{2,1,0:T(8,128)(2,1)} %copy-done), calls=%async_computation.3 | async-start | bytes 4194304 | tf_op jit(solution)/shard_map/all_to_all | solution.py:220
  84.9 6.3 %collective-permute-start = (bf16[192,4096]{1,0:T(8,128)(2,1)}, bf16[192,4096]{1,0:T(8,128)(2,1)S(1)}, u32[]{:S(2)}, u32[]{:S(2)}) collective-permute-start(bf16[192,4096]{1,0:T(8,128)(2,1)} %refs_0_.1), channel_id=1, source_target_pairs={{0,16},{16,0},{1,17},{17,1},{2,18},{18,2},{3,19},{19,3},{4,20},{20... | collective-permute-start | bytes 4718600 | tf_op jit(solution)/shard_map/ppermute | solution.py:255
  86.8 5.8 %collective-permute-start.1 = (bf16[192,4096]{1,0:T(8,128)(2,1)}, bf16[192,4096]{1,0:T(8,128)(2,1)S(1)}, u32[]{:S(2)}, u32[]{:S(2)}) collective-permute-start(bf16[192,4096]{1,0:T(8,128)(2,1)} %refs_1_.1), channel_id=1, source_target_pairs={{0,16},{16,0},{1,17},{17,1},{2,18},{18,2},{3,19},{19,3},{4,20},{20... | collective-permute-start | bytes 4718600 | tf_op jit(solution)/shard_map/ppermute | solution.py:255
  89.2 5.8 %collective-permute-start.2 = (bf16[16,384,128]{2,1,0:T(8,128)(2,1)}, bf16[16,384,128]{2,1,0:T(8,128)(2,1)}, u32[]{:S(2)}, u32[]{:S(2)}) collective-permute-start(bf16[16,384,128]{2,1,0:T(8,128)(2,1)} %copy-done.4), channel_id=1, source_target_pairs={{0,16},{16,0},{1,17},{17,1},{2,18},{18,2},{3,19},{19,3},{4,20},{20... | collective-permute-start | bytes 4718600 | tf_op jit(solution)/shard_map/ppermute | solution.py:255
  91.2 1.5 copy-start.5
  92.7 1.2 copy-start.6
